TPU v7x, 128 devices: a whole 4x4x4 slice. The times are simulated.
128 devices in a mesh: band: 8 (over z, core), patch: 16 (over y, x).
Axes of the slice: x: 4, y: 4, z: 4, core: 2. Of those that a mesh axis runs over, the one named last changes fastest.
Arguments:
- grid_feats: bfloat16 [262144, 227], P(('band', 'patch')), may hold values from -6 to 6
- mesh_feats: bfloat16 [32768, 512], P(('band', 'patch')), may hold values from -6 to 6
- cotangent: bfloat16 [32768, 512], P(('band', 'patch')), may hold values from -6 to 6
- w_embed: bfloat16 [227, 512], replicated, may hold values from -0.375 to 0.375
- w_send: bfloat16 [512, 512], replicated, may hold values from -0.25 to 0.25
- w_recv: bfloat16 [512, 512], replicated, may hold values from -0.25 to 0.25
- w_out: bfloat16 [512, 512], replicated, may hold values from -0.0625 to 0.0625
- u_src: bfloat16 [256, 512], replicated, may hold values from -0.375 to 0.375
- u_dst: bfloat16 [256, 512], replicated, may hold values from -0.375 to 0.375
- u_out: bfloat16 [512, 256], replicated, may hold values from -0.09375 to 0.09375
- v_in: bfloat16 [256, 512], replicated, may hold values from -0.375 to 0.375
- v_out: bfloat16 [512, 256], replicated, may hold values from -0.25 to 0.25
- send_rows: int32 [128, 2048], P(('band', 'patch')), may hold values from 0 to 2047, as said below
- enc_src: int32 [128, 4096], P(('band', 'patch')), may hold values from 0 to 2047, as said below
- enc_dst: int32 [128, 4096], P(('band', 'patch')), may hold values from -1 to 255, as said below
- halo_send: int32 [128, 2, 2, 32], P(('band', 'patch')), may hold values from 0 to 255, as said below
- mesh_src: int32 [128, 2048], P(('band', 'patch')), may hold values from 0 to 383, as said below
- mesh_dst: int32 [128, 2048], P(('band', 'patch')), may hold values from -1 to 255, as said below
Outputs:
- grid_grad: bfloat16 [262144, 227], P(('band', 'patch'))
- mesh_grad: float32 [32768, 512], P(('band', 'patch'))
- grad_w_embed: float32 [227, 512], replicated
- grad_w_send: float32 [512, 512], replicated
- grad_w_recv: float32 [512, 512], replicated
- grad_w_out: float32 [512, 512], replicated
- grad_u_src: float32 [256, 512], replicated
- grad_u_dst: float32 [256, 512], replicated
- grad_u_out: float32 [512, 256], replicated
- grad_v_in: float32 [256, 512], replicated
- grad_v_out: float32 [512, 256], replicated
Inputs may be any that keep to these rules, and one draw needn't show every extreme that they name: Each send_rows[d] names each of the device's 2048 local grid rows exactly once. `enc_src`: index into the device's received grid rows; the first 2048 slots name each received row once and are live. `enc_dst`: local mesh node of a live slot, -1 for an empty slot; empty slots follow all live ones of a device; some device has all 4096 slots live. halo_send[d, 0, 0] and [d, 0, 1] go to the band neighbour below and above, [d, 1, 0] and [d, 1, 1] to the patch neighbours below and above. `mesh_src`: row of the halo table: own 256 nodes, then the blocks from band - 1, band + 1, patch - 1, patch + 1; the first 128 slots name each received row once and are live. `mesh_dst`: local receiver of a live slot, -1 for an empty slot; empty slots follow all live ones of a device; some device has all 2048 slots live.
All inputs are finite; a program needn't handle non-finite values.
Results may differ from a plain program's by a relative error of at most 0.025.
Values may be sent and summed in bfloat16 or wider, within the bound.
No kernel may reach another device: no remote copies, remote signals or barrier semaphores. Data moves between devices by JAX's collectives and lax.ppermute only.
A program may use at most 128 MiB of HBM per device.

v0:
```python
import functools

import jax
import jax.numpy as jnp
from jax import lax
from jax.experimental import pallas as pl
from jax.experimental.pallas import tpu as pltpu
from jax.sharding import Mesh
from jax.sharding import PartitionSpec as P

BF16 = jnp.bfloat16
F32 = jnp.float32
LANES = 128
EDGE_TILE = 1024
ROW_TILE = 512
VMEM_LIMIT = 32 * 1024 * 1024
PIECES = 4
BAND = ("z", "core")
PATCH = ("y", "x")


def mm(left, right):
    return lax.dot_general(left, right, (((1,), (0,)), ((), ())), preferred_element_type=F32)


def mm_left(left, right):
    return lax.dot_general(left, right, (((0,), (0,)), ((), ())), preferred_element_type=F32)


def mm_right(left, right):
    return lax.dot_general(left, right, (((1,), (1,)), ((), ())), preferred_element_type=F32)


def table_by_row(index, count):
    n = index.shape[1]
    rows = lax.broadcasted_iota(jnp.int32, (count, n), 0)
    return jnp.where(rows == index, 1.0, 0.0).astype(BF16)


def table_by_column(index, count):
    n = index.shape[1]
    parts = []
    for start in range(0, n, LANES):
        width = min(LANES, n - start)
        piece = jnp.broadcast_to(index[:, start : start + width], (LANES, width))
        column = jnp.transpose(piece)
        wide = jnp.concatenate([column] * (count // LANES), axis=1)
        columns = lax.broadcasted_iota(jnp.int32, (width, count), 1)
        parts.append(jnp.where(wide == columns, 1.0, 0.0).astype(BF16))
    return parts[0] if len(parts) == 1 else jnp.concatenate(parts, axis=0)


def table_by_wide(column, count):
    wide = jnp.concatenate([column.astype(F32)] * (count // LANES), axis=1)
    columns = lax.broadcasted_iota(jnp.int32, wide.shape, 1).astype(F32)
    return jnp.where(wide == columns, 1.0, 0.0).astype(BF16)


def tiles(stop, size, body):
    def step(i, carry):
        body(pl.multiple_of(i * size, size))
        return carry

    lax.fori_loop(0, stop // size, step, 0)


def silu_both(value):
    sigma = 0.5 * jnp.tanh(0.5 * value) + 0.5
    act = value * sigma
    return act, sigma + act * (1.0 - sigma)


class Sent:
    def __init__(self, target, buffer, semaphores):
        self.target, self.buffer, self.semaphores = target, buffer, semaphores
        self.shape = buffer.shape
        self.copies = []

    def __setitem__(self, index, value):
        self.buffer[index] = value

    def __getitem__(self, index):
        return self.buffer[index]

    def send(self, start=0, count=None):
        rows = pl.ds(start, self.shape[0] if count is None else count)
        copy = pltpu.make_async_copy(self.buffer.at[rows], self.target.at[rows], self.semaphores.at[len(self.copies)])
        copy.start()
        self.copies.append(copy)


def call(kernel, out_shape, work, args, scalars=0, sent=(), scratch=()):
    outs = list(out_shape)
    buffers = [pltpu.VMEM(outs[k].shape, outs[k].dtype) for k in sent]
    buffers += [pltpu.SemaphoreType.DMA((PIECES,)) for _ in sent]

    def run(*refs):
        ins, results, rest = refs[: len(args)], list(refs[len(args) : len(args) + len(outs)]), refs[len(args) + len(outs) :]
        for k, place in enumerate(sent):
            results[place] = Sent(results[place], rest[k], rest[len(sent) + k])
        kernel(*ins, *results, *rest[len(buffers) :])
        for place in sent:
            for copy in results[place].copies:
                copy.wait()

    spaces = [pltpu.SMEM] * scalars + [pltpu.VMEM] * (len(args) - scalars)
    return pl.pallas_call(
        run,
        out_shape=outs,
        in_specs=[pl.BlockSpec(memory_space=space) for space in spaces],
        out_specs=[pl.BlockSpec(memory_space=pl.ANY if k in sent else pltpu.VMEM) for k in range(len(outs))],
        scratch_shapes=buffers + list(scratch),
        cost_estimate=pl.CostEstimate(flops=int(work * 1e9), bytes_accessed=int(work * 1e6), transcendentals=0),
        compiler_params=pltpu.CompilerParams(vmem_limit_bytes=VMEM_LIMIT),
    )(*args)


def shape(dims, kind):
    return jax.ShapeDtypeStruct(tuple(dims), kind)


def pick_rim_kernel(order_ref, grid_ref, *out_refs):
    rim = out_refs[0].shape[1]
    keep = order_ref.shape[1] - 4 * rim
    table = table_by_row(order_ref[:, keep:], grid_ref.shape[1])
    picked = mm(grid_ref[...], table).astype(BF16)
    for k in range(4):
        out_refs[k][...] = picked[:, k * rim : (k + 1) * rim]


def keep_kernel(
    order_ref, src_ref, dst_ref, grid_ref, mesh_ref, embed_ref, send_ref, recv_ref,
    rows_ref, sender_ref, node_ref, column_ref, row_ref, dst_s,
):
    keep = rows_ref.shape[1]
    rows = order_ref.shape[1]
    for start in range(0, rows, LANES):
        piece = jnp.broadcast_to(dst_ref[:, start : start + LANES], (LANES, LANES))
        dst_s[start : start + LANES, :] = jnp.transpose(piece).astype(F32).astype(BF16)
    first = src_ref[:, 0:rows]


    def sort(start):
        ids = lax.broadcasted_iota(jnp.int32, (ROW_TILE, rows), 0) + start
        table = jnp.where(ids == first, 1.0, 0.0).astype(BF16)
        column = mm(table, dst_s[...])
        column_ref[pl.ds(start, ROW_TILE), :] = column.astype(BF16)
        for k in range(0, ROW_TILE, LANES):
            turned = jnp.transpose(column[k : k + LANES, :])
            row_ref[:, pl.ds(pl.multiple_of(start + k, LANES), LANES)] = turned[0:1, :].astype(jnp.int32)

    tiles(rows, ROW_TILE, sort)
    for start in range(0, keep, ROW_TILE):
        stop = start + ROW_TILE
        table = table_by_row(order_ref[:, start:stop], grid_ref.shape[1])
        cols = mm(grid_ref[...], table).astype(BF16)
        rows_ref[:, start:stop] = cols
        embedded = silu_both(mm_left(cols, embed_ref[...]))[0].astype(BF16)
        sender_ref[start:stop, :] = mm(embedded, send_ref[...]).astype(BF16)
    node_ref[...] = mm(mesh_ref[...], recv_ref[...]).astype(BF16)


def encode_kernel(
    flag_ref, src_ref, dst_ref, row_ref, halo_ref, in0, in1, in2, in3, own0, own1, embed_ref, send_ref,
    sender_ref, node_ref, column_ref, out_w_ref, mesh_ref,
    rim_ref, slope0, slope1, gathered_ref, latent_ref, h00, h01, h10, h11,
    table, total,
):
    keep = sender_ref.shape[0]
    rim = in0.shape[1]
    rows = keep + 4 * rim
    nodes = node_ref.shape[0]
    rim_ref[:, 0:rim] = jnp.where(flag_ref[0] > 0, in0[...], own0[...])
    rim_ref[:, rim : 2 * rim] = jnp.where(flag_ref[1] > 0, in1[...], own1[...])
    rim_ref[:, 2 * rim : 3 * rim] = in2[...]
    rim_ref[:, 3 * rim : 4 * rim] = in3[...]
    embedded = silu_both(mm_left(rim_ref[...], embed_ref[...]))[0].astype(BF16)
    table[keep:rows, :] = mm(embedded, send_ref[...]).astype(BF16)
    table[0:keep, :] = sender_ref[...]
    table[rows : rows + nodes, :] = node_ref[...]
    for start in range(0, src_ref.shape[1], EDGE_TILE):
        stop = start + EDGE_TILE
        if start < rows:
            node = mm(table_by_wide(column_ref[start:stop, :], nodes), node_ref[...])
            value = table[start:stop, :].astype(F32) + node
            by_row = table_by_row(row_ref[:, start:stop], nodes)
        else:
            src = src_ref[:, start:stop]
            dst = dst_ref[:, start:stop]
            both = jnp.concatenate([table_by_column(src, rows), table_by_column(dst, nodes)], axis=1)
            value = mm(both, table[...])
            by_row = table_by_row(dst, nodes)
        act, slope = silu_both(value)
        ref, base = (slope0, 0) if start < rows else (slope1, rows)
        ref[start - base : stop - base, :] = slope.astype(BF16)
        part = mm(by_row, act.astype(BF16))
        total[...] = part if start == 0 else total[...] + part
    gathered = total[...].astype(BF16)
    gathered_ref[...] = gathered
    latent = (mesh_ref[...].astype(F32) + mm(gathered, out_w_ref[...])).astype(BF16)
    latent_ref[...] = latent
    lower = latent[:, latent.shape[1] // 2 :]
    for a, b, ref in ((0, 0, h00), (0, 1, h01), (1, 0, h10), (1, 1, h11)):
        pick = table_by_row(halo_ref[0, a, b : b + 1, :], nodes)
        ref[...] = mm_left(pick, lower).astype(BF16)


def mesh_kernel(
    flag_ref, src_ref, dst_ref, latent_ref, cot_ref, b0, b1, b2, b3, u_src_ref, u_dst_ref, u_out_ref, v_in_ref, v_out_ref,
    g0, g1, g2, g3, coupled_grad_ref, lower_grad_ref, halo_table_ref, ends_ref, summed_ref, coupled_ref, hidden_ref, hidden_grad_ref,
    table, slope_s, total, ends,
):
    nodes = latent_ref.shape[0]
    half = latent_ref.shape[1] // 2
    width = b0.shape[0]
    rows = nodes + 4 * width
    upper = latent_ref[:, :half]
    lower = latent_ref[:, half:]
    halo_table_ref[0:nodes, :] = lower
    for k, ref in enumerate((b0, b1, b2, b3)):
        value = ref[...] if k > 1 else jnp.where(flag_ref[k] > 0, ref[...], jnp.zeros_like(ref[...]))
        halo_table_ref[nodes + k * width : nodes + (k + 1) * width, :] = value
    table[0:rows, :] = mm(halo_table_ref[...], u_src_ref[...]).astype(BF16)
    table[rows : rows + nodes, :] = mm(lower, u_dst_ref[...]).astype(BF16)
    for start in range(0, src_ref.shape[1], EDGE_TILE):
        stop = start + EDGE_TILE
        src = src_ref[:, start:stop]
        dst = dst_ref[:, start:stop]
        both = jnp.concatenate([table_by_column(src, rows), table_by_column(dst, nodes)], axis=1)
        act, slope = silu_both(mm(both, table[...]))
        slope_s[start:stop, :] = slope.astype(BF16)
        part = mm(table_by_row(dst, nodes), act.astype(BF16))
        total[...] = part if start == 0 else total[...] + part
    summed = total[...].astype(BF16)
    summed_ref[...] = summed
    coupled = (upper.astype(F32) + mm(summed, u_out_ref[...])).astype(BF16)
    coupled_ref[...] = coupled
    act, slope = silu_both(mm(coupled, v_in_ref[...]))
    hidden_ref[...] = act.astype(BF16)
    upper_cot = cot_ref[:, :half]
    lower_cot = cot_ref[:, half:]
    hidden_grad = (mm_right(lower_cot, v_out_ref[...]) * slope).astype(BF16)
    hidden_grad_ref[...] = hidden_grad
    coupled_grad = (upper_cot.astype(F32) + mm_right(hidden_grad, v_in_ref[...])).astype(BF16)
    coupled_grad_ref[...] = coupled_grad
    summed_grad = mm_right(coupled_grad, u_out_ref[...]).astype(BF16)

    for start in range(0, src_ref.shape[1], EDGE_TILE):
        stop = start + EDGE_TILE
        src = src_ref[:, start:stop]
        dst = dst_ref[:, start:stop]
        grad = mm(table_by_column(dst, nodes), summed_grad) * slope_s[start:stop, :].astype(F32)
        both = jnp.concatenate([table_by_row(src, rows), table_by_row(dst, nodes)], axis=0)
        part = mm(both, grad.astype(BF16))
        ends[...] = part if start == 0 else ends[...] + part
    ends_ref[...] = ends[...].astype(BF16)
    source_grad = ends_ref[0:rows, :]
    target_grad = ends_ref[rows : rows + nodes, :]
    table_grad = mm_right(source_grad, u_src_ref[...])
    lower_grad_ref[...] = lower_cot.astype(F32) + mm_right(target_grad, u_dst_ref[...]) + table_grad[0:nodes, :]
    for k, ref in enumerate((g0, g1, g2, g3)):
        ref[...] = table_grad[nodes + k * width : nodes + (k + 1) * width, :].astype(BF16)


def store_halves(core_ref, mine_ref, other_ref, start, value):
    half = mine_ref.shape[0]
    value = value.astype(BF16)
    done = 0
    while done < value.shape[0]:
        row = start + done
        count = min(value.shape[0] - done, half - row % half)
        piece = value[done : done + count, :]
        here = row % half

        @pl.when(core_ref[0] == row // half)
        def _(piece=piece, here=here, count=count):
            mine_ref[here : here + count, :] = piece

        @pl.when(core_ref[0] != row // half)
        def _(piece=piece, here=here, count=count):
            other_ref[here : here + count, :] = piece

        done += count


def side_by_side(value):
    rows = value.shape[0] // 2
    return jnp.concatenate([value[:rows, :], value[rows:, :]], axis=1)


def mesh_weight_kernel(
    core_ref, halo_table_ref, ends_ref, summed_ref, coupled_ref, hidden_ref, hidden_grad_ref, coupled_grad_ref, cot_ref,
    mine_ref, other_ref,
):
    rows = halo_table_ref.shape[0]
    nodes, half = coupled_ref.shape
    parts = (
        mm_left(halo_table_ref[...], ends_ref[0:rows, :]),
        mm_left(halo_table_ref[0:nodes, :], ends_ref[rows : rows + nodes, :]),
        side_by_side(mm_left(summed_ref[...], coupled_grad_ref[...])),
        mm_left(coupled_ref[...], hidden_grad_ref[...]),
        side_by_side(mm_left(hidden_ref[...], cot_ref[:, half:])),
    )
    start = 0
    for part in parts:
        store_halves(core_ref, mine_ref, other_ref, start, part)
        start += part.shape[0]


def encoder_back_kernel(
    core_ref, flag_ref, src_ref, dst_ref, row_ref, halo_ref, r0, r1, r2, r3, lower_grad_ref, coupled_grad_ref, out_w_ref,
    column_ref, slope0, slope1, gathered_ref, recv_ref, mesh_ref, rim_rows_ref, embed_ref, send_ref, keep_rows_ref,
    keep_grad_ref, g0, g1, g2, g3, mesh_grad_ref, mine_ref, other_ref,
    edge_s, latent_s, nodes_s, sum_send, sum_embed,
):
    nodes, dim = mesh_ref.shape
    keep = keep_rows_ref.shape[1]
    rim = g0.shape[1]
    lower_grad = lower_grad_ref[...]
    for a, b, ref in ((0, 0, r0), (0, 1, r1), (1, 0, r2), (1, 1, r3)):
        value = ref[...] if a else jnp.where(flag_ref[b] > 0, ref[...], jnp.zeros_like(ref[...]))
        lower_grad += mm(table_by_row(halo_ref[0, a, b : b + 1, :], nodes), value)
    half = lower_grad.shape[1]
    latent_s[:, :half] = coupled_grad_ref[...]
    latent_s[:, half:] = lower_grad.astype(BF16)
    latent_grad = latent_s[...]
    gathered_grad = mm_right(latent_grad, out_w_ref[...]).astype(BF16)
    rows = column_ref.shape[0]
    for start in range(0, src_ref.shape[1], EDGE_TILE):
        stop = start + EDGE_TILE
        if start < rows:
            by_column = table_by_wide(column_ref[start:stop, :], nodes)
            by_row = table_by_row(row_ref[:, start:stop], nodes)
            slope = slope0[start:stop, :]
        else:
            dst = dst_ref[:, start:stop]
            by_column = table_by_column(dst, nodes)
            by_row = table_by_row(dst, nodes)
            slope = slope1[start - rows : stop - rows, :]
        grad = (mm(by_column, gathered_grad) * slope.astype(F32)).astype(BF16)
        edge_s[start:stop, :] = grad
        part = mm(by_row, grad)
        nodes_s[...] = part if start == 0 else nodes_s[...] + part
    store_halves(core_ref, mine_ref, other_ref, 0, mm_left(gathered_ref[...], latent_grad))
    node_grad = nodes_s[...].astype(BF16)
    store_halves(core_ref, mine_ref, other_ref, dim, mm_left(mesh_ref[...], node_grad))
    mesh_grad_ref[...] = latent_grad.astype(F32) + mm_right(node_grad, recv_ref[...])
    mesh_grad_ref.send()
    extra = src_ref[:, rows:]

    def back(cols, start, count):
        ids = lax.broadcasted_iota(jnp.int32, (count, extra.shape[1]), 0) + start
        table = jnp.where(ids == extra, 1.0, 0.0).astype(BF16)
        own = edge_s[pl.ds(start, count), :].astype(F32)
        sender_grad = (own + mm(table, edge_s[rows:, :])).astype(BF16)
        act, slope = silu_both(mm_left(cols, embed_ref[...]))
        embedded_grad = mm_right(sender_grad, send_ref[...]).astype(BF16)
        embed_grad = (embedded_grad.astype(F32) * slope).astype(BF16)
        cols_grad = mm_right(embed_ref[...], embed_grad).astype(BF16)
        return cols_grad, mm_left(act.astype(BF16), sender_grad), mm(cols, embed_grad)

    rim_grad, send_part, embed_part = back(rim_rows_ref[...], keep, 4 * rim)
    sum_send[...] = send_part
    sum_embed[...] = embed_part
    for k, ref in enumerate((g0, g1, g2, g3)):
        ref[...] = rim_grad[:, k * rim : (k + 1) * rim]

    def kept(start):
        here = pl.ds(start, ROW_TILE)
        cols_grad, send_part, embed_part = back(keep_rows_ref[:, here], start, ROW_TILE)
        keep_grad_ref[:, here] = cols_grad
        sum_send[...] += send_part
        sum_embed[...] += embed_part

    tiles(keep, ROW_TILE, kept)
    store_halves(core_ref, mine_ref, other_ref, 2 * dim, sum_send[...])
    grad_embed = sum_embed[...]
    pad = jnp.zeros((half - grad_embed.shape[0], dim), F32)
    store_halves(core_ref, mine_ref, other_ref, 3 * dim, jnp.concatenate([grad_embed, pad], axis=0))


def place_kernel(flag_ref, order_ref, keep_ref, in0, in1, in2, in3, own0, own1, grid_grad_ref, all_s):
    keep = keep_ref.shape[1]
    rim = in0.shape[1]
    all_s[:, 0:keep] = keep_ref[...]
    all_s[:, keep : keep + rim] = jnp.where(flag_ref[0] > 0, in0[...], own0[...])
    all_s[:, keep + rim : keep + 2 * rim] = jnp.where(flag_ref[1] > 0, in1[...], own1[...])
    all_s[:, keep + 2 * rim : keep + 3 * rim] = in2[...]
    all_s[:, keep + 3 * rim : keep + 4 * rim] = in3[...]


    def place(start):
        ids = lax.broadcasted_iota(jnp.int32, (ROW_TILE, order_ref.shape[1]), 0) + start
        table = jnp.where(ids == order_ref[...], 1.0, 0.0).astype(BF16)
        grid_grad_ref[:, pl.ds(start, ROW_TILE)] = mm_right(all_s[...], table).astype(BF16)

    tiles(grid_grad_ref.shape[1], ROW_TILE, place)


def unpack_kernel(a_rows, core_ref, mine_ref, other_ref, embed_ref, send_ref, recv_ref, out_ref, u_src_ref, u_dst_ref, u_out_ref, v_in_ref, v_out_ref):
    first = core_ref[0] == 0

    def read(base, half, start, count):
        pieces = []
        while count > 0:
            here = start % half
            some = min(count, half - here)
            mine = mine_ref[base + here : base + here + some, :]
            other = other_ref[base + here : base + here + some, :]
            pieces.append(jnp.where(first == (start < half), mine, other))
            start += some
            count -= some
        value = pieces[0] if len(pieces) == 1 else jnp.concatenate(pieces, axis=0)
        return value.astype(F32)

    dim, half = v_out_ref.shape
    a_half = a_rows // 2
    b_half = mine_ref.shape[0] - a_half
    for start, ref in ((0, u_src_ref), (half, u_dst_ref), (3 * half, v_in_ref)):
        ref[...] = read(0, a_half, start, half)
        ref.send()
    for start, ref in ((2 * half, u_out_ref), (4 * half, v_out_ref)):
        value = read(0, a_half, start, half)
        ref[0:half, :] = value[:, :half]
        ref[half:, :] = value[:, half:]
        ref.send()
    for start, ref in ((0, out_ref), (dim, recv_ref), (2 * dim, send_ref)):
        ref[...] = read(a_half, b_half, start, dim)
        ref.send()
    ref = embed_ref
    ref[...] = read(a_half, b_half, 3 * dim, half)[0 : ref.shape[0], :]
    ref.send()


def trade(below, above, west, east):
    bands = lax.axis_size(BAND)
    patches = lax.axis_size(PATCH)
    up = [(i, (i + 1) % bands) for i in range(bands)]
    down = [((i + 1) % bands, i) for i in range(bands)]
    right = [(i, (i + 1) % patches) for i in range(patches)]
    left = [((i + 1) % patches, i) for i in range(patches)]
    return (
        lax.ppermute(above, BAND, up),
        lax.ppermute(below, BAND, down),
        lax.ppermute(east, PATCH, right),
        lax.ppermute(west, PATCH, left),
    )


def swap_cores(value):
    return lax.ppermute(value, "core", [(0, 1), (1, 0)])


def body(
    grid_feats, mesh_feats, cotangent, w_embed, w_send, w_recv, w_out, u_src, u_dst, u_out, v_in, v_out,
    send_rows, enc_src, enc_dst, halo_send, mesh_src, mesh_dst,
):
    chans = grid_feats.shape[1]
    grid_rows = grid_feats.shape[0]
    nodes, dim = mesh_feats.shape
    half = dim // 2
    rim = grid_rows // 16
    keep = grid_rows - 4 * rim
    edges = enc_src.shape[1]
    width = halo_send.shape[3]
    table_rows = nodes + 4 * width
    band = lax.axis_index(BAND)
    flags = jnp.stack([band, lax.axis_size(BAND) - 1 - band]).astype(jnp.int32)
    core = lax.axis_index("core").astype(jnp.int32).reshape(1)

    grid_cols = grid_feats.T
    own = call(pick_rim_kernel, [shape((chans, rim), BF16)] * 4, 1, (send_rows, grid_cols))
    arrived = trade(*own)
    outs = [
        shape((chans, keep), BF16), shape((keep, dim), BF16), shape((nodes, dim), BF16),
        shape((grid_rows, LANES), BF16), shape((1, grid_rows), jnp.int32),
    ]
    ins = (send_rows, enc_src, enc_dst, grid_cols, mesh_feats, w_embed, w_send, w_recv)
    keep_rows, keep_sender, node_part, column, row = call(
        keep_kernel, outs, 6, ins, scratch=[pltpu.VMEM((grid_rows, LANES), BF16)]
    )

    outs = [
        shape((chans, 4 * rim), BF16), shape((grid_rows, dim), BF16), shape((edges - grid_rows, dim), BF16),
        shape((nodes, dim), BF16), shape((nodes, dim), BF16),
    ] + [shape((width, half), BF16)] * 4
    ins = (
        flags, enc_src, enc_dst, row, halo_send, *arrived, own[0], own[1], w_embed, w_send,
        keep_sender, node_part, column, w_out, mesh_feats,
    )
    rim_rows, slope0, slope1, gathered, latent, h00, h01, h10, h11 = call(
        encode_kernel, outs, 12, ins, scalars=1,
        scratch=[pltpu.VMEM((grid_rows + nodes, dim), BF16), pltpu.VMEM((nodes, dim), F32)],
    )

    halos = trade(h00, h01, h10, h11)
    outs = [shape((width, half), BF16)] * 4 + [
        shape((nodes, half), BF16), shape((nodes, half), F32), shape((table_rows, half), BF16),
        shape((table_rows + nodes, dim), BF16), shape((nodes, dim), BF16), shape((nodes, half), BF16),
        shape((nodes, dim), BF16), shape((nodes, dim), BF16),
    ]
    ins = (flags, mesh_src, mesh_dst, latent, cotangent, *halos, u_src, u_dst, u_out, v_in, v_out)
    (g0, g1, g2, g3, coupled_grad, lower_grad, halo_table, ends, summed, coupled, hidden, hidden_grad) = call(
        mesh_kernel, outs, 6, ins, scalars=1,
        scratch=[
            pltpu.VMEM((table_rows + nodes, dim), BF16), pltpu.VMEM((mesh_src.shape[1], dim), BF16),
            pltpu.VMEM((nodes, dim), F32), pltpu.VMEM((table_rows + nodes, dim), F32),
        ],
    )
    returned = trade(g0, g1, g2, g3)
    a_rows = 5 * half
    ins = (core, halo_table, ends, summed, coupled, hidden, hidden_grad, coupled_grad, cotangent)
    a_mine, a_other = call(mesh_weight_kernel, [shape((a_rows // 2, dim), BF16)] * 2, 1, ins, scalars=1)
    a_in = swap_cores(a_other)
    lower_grad, a_mine = lax.optimization_barrier((lower_grad, a_mine))

    b_rows = 3 * dim + half
    outs = [shape((chans, keep), BF16)] + [shape((chans, rim), BF16)] * 4 + [shape((nodes, dim), F32)]
    outs += [shape((b_rows // 2, dim), BF16)] * 2
    ins = (
        core, flags, enc_src, enc_dst, row, halo_send, *returned, lower_grad, coupled_grad, w_out,
        column, slope0, slope1, gathered, w_recv, mesh_feats, rim_rows, w_embed, w_send, keep_rows,
    )
    keep_grad, q0, q1, q2, q3, mesh_grad, b_mine, b_other = call(
        encoder_back_kernel, outs, 14, ins, scalars=2, sent=(5,),
        scratch=[
            pltpu.VMEM((edges, dim), BF16), pltpu.VMEM((nodes, dim), BF16), pltpu.VMEM((nodes, dim), F32),
            pltpu.VMEM((dim, dim), F32), pltpu.VMEM((chans, dim), F32),
        ],
    )
    b_in = swap_cores(b_other)
    back = trade(q0, q1, q2, q3)
    patches = lax.axis_size(PATCH)
    packed = (a_rows + b_rows) // 2
    pair = jnp.concatenate([a_mine.astype(F32) + a_in.astype(F32), b_mine.astype(F32) + b_in.astype(F32)], axis=0)
    pair = pair.astype(BF16).reshape(patches, packed // patches, dim)
    pair, *back = lax.optimization_barrier((pair, *back))
    parts = lax.all_to_all(pair, PATCH, 0, 0)
    part = jnp.sum(parts.astype(F32), axis=0).astype(BF16)
    away = [part] + [lax.ppermute(part, "z", [(i, (i + k) % 4) for i in range(4)]) for k in (1, 2, 3)]
    away = [piece.astype(F32) for piece in away]
    total = ((away[0] + away[2]) + (away[1] + away[3])).astype(BF16)
    mine = lax.all_to_all(jnp.broadcast_to(total[None], parts.shape), PATCH, 0, 0).reshape(packed, dim)
    other = swap_cores(mine)
    ins = (flags, send_rows, keep_grad, *back, q0, q1)
    (grid_grad,) = call(
        place_kernel, [shape((chans, grid_rows), BF16)], 5, ins, scalars=1, scratch=[pltpu.VMEM((chans, grid_rows), BF16)]
    )
    outs = [shape((chans, dim), F32)] + [shape((dim, dim), F32)] * 3 + [shape((half, dim), F32)] * 2
    outs += [shape((dim, half), F32), shape((half, dim), F32), shape((dim, half), F32)]
    totals = call(functools.partial(unpack_kernel, a_rows), outs, 4, (core, mine, other), scalars=1, sent=tuple(range(9)))
    return (grid_grad.T, mesh_grad, *totals)


def solution(mesh):
    chips = Mesh(mesh.devices.reshape(mesh.shape["band"] // 2, 2, 4, mesh.shape["patch"] // 4), ("z", "core", "y", "x"))
    everywhere = BAND + PATCH
    rows = P(everywhere, None)
    in_specs = (rows,) * 3 + (P(),) * 9 + (rows,) * 3 + (P(everywhere, None, None, None),) + (rows,) * 2
    out_specs = (rows,) * 2 + (P(),) * 9
    return jax.shard_map(body, mesh=chips, in_specs=in_specs, out_specs=out_specs, check_vma=False)
```

profile of v0, /device:TPU:1, one launch (start us, length us, event | category | flops | bytes accessed | tf_op | source)
XLA Modules:
  0.0 152.6 jit_solution(98676844810443549)
XLA Ops:
  0.7 1.2 copy-done
  1.8 0.7 copy-done.17
  2.6 0.7 shard_map.258
  3.3 3.0 %collective-permute-start = (bf16[227,128]{1,0:T(8,128)(2,1)S(1)}, bf16[227,128]{1,0:T(8,128)(2,1)S(1)}, u32[]{:S(2)}, u32[]{:S(2)}) collective-permute-start(bf16[227,128]{1,0:T(8,128)(2,1)S(1)} %get-tuple-element.68.refs_10_), channel_id=1, source_target_pairs={{0,16},{16,32},{32,48},{48,64},{64,80},{80,96},{96,112},{112,0},{1... | collective-permute-start | bytes 174344 | tf_op jit(solution)/shard_map/ppermute | solution.py:443
  6.3 1.2 collective-permute-start.2
  7.5 3.7 %collective-permute-start.3 = (bf16[227,128]{1,0:T(8,128)(2,1)S(1)}, bf16[227,128]{1,0:T(8,128)(2,1)S(1)}, u32[]{:S(2)}, u32[]{:S(2)}) collective-permute-start(bf16[227,128]{1,0:T(8,128)(2,1)S(1)} %get-tuple-element.71), channel_id=1, source_target_pairs={{1,0},{2,1},{3,2},{4,3},{5,4},{6,5},{7,6},{8,7},{9,8},{10,9},{11,1... | collective-permute-start | bytes 174344 | tf_op jit(solution)/shard_map/ppermute | solution.py:446
  11.3 0.0 copy-start.4
  11.3 0.0 copy-start.19
  11.3 7.2 %shard_map.257 = (bf16[227,1536]{1,0:T(8,128)(2,1)S(1)}, bf16[1536,512]{1,0:T(8,128)(2,1)S(1)}, bf16[256,512]{1,0:T(8,128)(2,1)S(1)}, bf16[2048,128]{1,0:T(8,128)(2,1)S(1)}, s32[1,2048]{1,0:T(1,128)S(1)}) custom-call(s32[1,2048]{1,0:T(1,128)S(1)} %copy-done.18, s32[1,4096]{1,0:T(1,128)S(1)} %copy-done.13, s32[1,4096]{1,0:T(1,128)S(1)} %copy-done.14, ...), custom_call_target="tpu_custom_call" | custom-call | flops 6000000000 | bytes 6000000 | tf_op jit(solution)/shard_map/pallas_call | solution.py:107
  18.5 0.1 pad_add_fusion.refs_0_.refs_1_
  18.7 0.0 copy-start.5
  18.7 0.0 copy-start.6
  18.7 0.0 copy-start.7
  18.7 0.0 copy-start.9
  18.7 0.0 copy-start.10
  18.8 10.2 %shard_map.259 = (bf16[227,512]{1,0:T(8,128)(2,1)S(1)}, bf16[2048,512]{1,0:T(8,128)(2,1)S(1)}, bf16[2048,512]{1,0:T(8,128)(2,1)S(1)}, bf16[256,512]{1,0:T(8,128)...) custom-call(s32[2]{0:T(128)S(1)} %pad_add_fusion.refs_0_.refs_1_, ...), custom_call_target="tpu_custom_call" | custom-call | flops 12000000000 | bytes 12000000 | tf_op jit(solution)/shard_map/pallas_call | solution.py:107
  28.9 2.2 %collective-permute-start.4 = (bf16[32,256]{1,0:T(8,128)(2,1)S(1)}, bf16[32,256]{1,0:T(8,128)(2,1)S(1)}, u32[]{:S(2)}, u32[]{:S(2)}) collective-permute-start(bf16[32,256]{1,0:T(8,128)(2,1)S(1)} %get-tuple-element.76), channel_id=1, source_target_pairs={{0,16},{16,32},{32,48},{48,64},{64,80},{80,96},{96,112},{112,0},{1... | collective-permute-start | bytes 49160 | tf_op jit(solution)/shard_map/ppermute | solution.py:443
  31.1 0.3 collective-permute-start.5
  31.4 4.8 %collective-permute-start.7 = (bf16[32,256]{1,0:T(8,128)(2,1)S(1)}, bf16[32,256]{1,0:T(8,128)(2,1)S(1)}, u32[]{:S(2)}, u32[]{:S(2)}) collective-permute-start(bf16[32,256]{1,0:T(8,128)(2,1)S(1)} %get-tuple-element.79), channel_id=1, source_target_pairs={{1,0},{2,1},{3,2},{4,3},{5,4},{6,5},{7,6},{8,7},{9,8},{10,9},{11,1... | collective-permute-start | bytes 49160 | tf_op jit(solution)/shard_map/ppermute | solution.py:446
  36.2 1.1 collective-permute-done.6.refs_7_
  37.3 6.7 %shard_map.260 = (bf16[32,256]{1,0:T(8,128)(2,1)S(1)}, bf16[32,256]{1,0:T(8,128)(2,1)S(1)}, bf16[32,256]{1,0:T(8,128)(2,1)S(1)}, bf16[32,256]{1,0:T(8,128)(2,1)S...) custom-call(s32[2]{0:T(128)S(1)} %pad_add_fusion.refs_0_.refs_1_, ...), custom_call_target="tpu_custom_call" | custom-call | flops 6000000000 | bytes 6000000 | tf_op jit(solution)/shard_map/pallas_call | solution.py:107
  44.1 0.1 collective-permute-start.10
  44.2 4.8 %collective-permute-start.11 = (bf16[32,256]{1,0:T(8,128)(2,1)S(1)}, bf16[32,256]{1,0:T(8,128)(2,1)S(1)}, u32[]{:S(2)}, u32[]{:S(2)}) collective-permute-start(bf16[32,256]{1,0:T(8,128)(2,1)S(1)} %get-tuple-element.83), channel_id=1, source_target_pairs={{1,0},{2,1},{3,2},{4,3},{5,4},{6,5},{7,6},{8,7},{9,8},{10,9},{11,1... | collective-permute-start | bytes 49160 | tf_op jit(solution)/shard_map/ppermute | solution.py:446
  49.0 3.2 %collective-permute-start.8 = (bf16[32,256]{1,0:T(8,128)(2,1)S(1)}, bf16[32,256]{1,0:T(8,128)(2,1)S(1)}, u32[]{:S(2)}, u32[]{:S(2)}) collective-permute-start(bf16[32,256]{1,0:T(8,128)(2,1)S(1)} %get-tuple-element.80), channel_id=1, source_target_pairs={{0,16},{16,32},{32,48},{48,64},{64,80},{80,96},{96,112},{112,0},{1... | collective-permute-start | bytes 49160 | tf_op jit(solution)/shard_map/ppermute | solution.py:443
  52.2 1.4 collective-permute-start.9
  53.7 0.8 shard_map.261
  54.5 3.0 %collective-permute-start.12 = (bf16[640,512]{1,0:T(8,128)(2,1)S(1)}, bf16[640,512]{1,0:T(8,128)(2,1)S(1)}, u32[]{:S(2)}, u32[]{:S(2)}) collective-permute-start(bf16[640,512]{1,0:T(8,128)(2,1)S(1)} %get-tuple-element.101), channel_id=1, source_target_pairs={{0,16},{16,0},{1,17},{17,1},{2,18},{18,2},{3,19},{19,3},{4,20},{20... | collective-permute-start | bytes 1966088 | tf_op jit(solution)/shard_map/ppermute | solution.py:451
  57.5 14.9 %shard_map.262 = (bf16[227,1536]{1,0:T(8,128)(2,1)S(1)}, bf16[227,128]{1,0:T(8,128)(2,1)S(1)}, bf16[227,128]{1,0:T(8,128)(2,1)S(1)}, bf16[227,128]{1,0:T(8,128)(...) custom-call(s32[1]{0:T(128)} %bitcast.2.refs_0_, ...), custom_call_target="tpu_custom_call" | custom-call | flops 14000000000 | bytes 14000000 | tf_op jit(solution)/shard_map/pallas_call | solution.py:107
  72.4 0.0 copy-start.20
  72.4 0.6 collective-permute-start.13
  73.0 0.5 collective-permute-start.15
  73.5 4.8 %collective-permute-start.17 = (bf16[227,128]{1,0:T(8,128)(2,1)S(1)}, bf16[227,128]{1,0:T(8,128)(2,1)S(1)}, u32[]{:S(2)}, u32[]{:S(2)}) collective-permute-start(bf16[227,128]{1,0:T(8,128)(2,1)S(1)} %get-tuple-element.107), channel_id=1, source_target_pairs={{1,0},{2,1},{3,2},{4,3},{5,4},{6,5},{7,6},{8,7},{9,8},{10,9},{11,1... | collective-permute-start | bytes 174344 | tf_op jit(solution)/shard_map/ppermute | solution.py:446
  78.3 0.2 add_convert_fusion.1
  78.5 0.3 add_convert_fusion
  78.8 0.1 pad_maximum_fusion
  78.9 1.0 collective-permute-done.16.refs_5_
  79.9 24.7 %all_to_all.10 = bf16[16,96,512]{2,1,0:T(8,128)(2,1)S(1)} all-to-all(bf16[16,96,512]{2,1,0:T(8,128)(2,1)S(1)} %bitcast.11), channel_id=1, replica_groups=mesh['z'=4,'core'=2,'y'=4,'x'=4] {'y','x'}, dimensions={0} | all-to-all | bytes 3145728 | tf_op jit(solution)/shard_map/all_to_all | solution.py:538
  104.6 0.2 reduce_sum.12
  104.8 7.1 %collective-permute-start.18 = (bf16[96,512]{1,0:T(8,128)(2,1)S(1)}, bf16[96,512]{1,0:T(8,128)(2,1)S(1)}, u32[]{:S(2)}, u32[]{:S(2)}) collective-permute-start(bf16[96,512]{1,0:T(8,128)(2,1)S(1)} %reduce_sum.12), channel_id=1, source_target_pairs={{0,64},{32,96},{64,0},{96,32},{1,65},{33,97},{65,1},{97,33},{2,66}... | collective-permute-start | bytes 294920 | tf_op jit(solution)/shard_map/ppermute | solution.py:540
  111.9 2.7 %collective-permute-start.20 = (bf16[96,512]{1,0:T(8,128)(2,1)S(1)}, bf16[96,512]{1,0:T(8,128)(2,1)S(1)}, u32[]{:S(2)}, u32[]{:S(2)}) collective-permute-start(bf16[96,512]{1,0:T(8,128)(2,1)S(1)} %reduce_sum.12), channel_id=1, source_target_pairs={{0,96},{32,0},{64,32},{96,64},{1,97},{33,1},{65,33},{97,65},{2,98}... | collective-permute-start | bytes 294920 | tf_op jit(solution)/shard_map/ppermute | solution.py:540
  114.6 2.5 %collective-permute-done.19 = bf16[96,512]{1,0:T(8,128)(2,1)S(1)} collective-permute-done((bf16[96,512]{1,0:T(8,128)(2,1)S(1)}, bf16[96,512]{1,0:T(8,128)(2,1)S(1)}, u32[]{:S(2)}, u32[]{:S(2)}) %collective-permute-start.19) | collective-permute-done | bytes 98336 | tf_op jit(solution)/shard_map/ppermute | solution.py:540
  117.1 0.1 add_convert_fusion.2
  117.2 0.1 broadcast_in_dim.2
  117.3 0.0 copy-start.21
  117.3 24.3 %all_to_all.11 = bf16[16,96,512]{2,1,0:T(8,128)(2,1)S(1)} all-to-all(bf16[16,96,512]{2,1,0:T(8,128)(2,1)S(1)} %broadcast_in_dim.2), channel_id=1, replica_groups=mesh['z'=4,'core'=2,'y'=4,'x'=4] {'y','x'}, dimensions={0} | all-to-all | bytes 3145728 | tf_op jit(solution)/shard_map/all_to_all | solution.py:543
  141.6 3.2 %collective-permute-start.21 = (bf16[1536,512]{1,0:T(8,128)(2,1)S(1)}, bf16[1536,512]{1,0:T(8,128)(2,1)S(1)}, u32[]{:S(2)}, u32[]{:S(2)}) collective-permute-start(bf16[1536,512]{1,0:T(8,128)(2,1)S(1)} %bitcast.7), channel_id=1, source_target_pairs={{0,16},{16,0},{1,17},{17,1},{2,18},{18,2},{3,19},{19,3},{4,20},{20... | collective-permute-start | bytes 4718600 | tf_op jit(solution)/shard_map/ppermute | solution.py:451
  144.8 4.6 %shard_map.263 = bf16[227,2048]{1,0:T(8,128)(2,1)} custom-call(s32[2]{0:T(128)S(1)} %pad_add_fusion.refs_0_.refs_1_, s32[1,2048]{1,0:T(1,128)S(1)} %copy-done.18, bf16[227,1536]{1,0:T(8,128)(2,1)S(1)} %copy-done.21, bf16[227,128]{1,0:T(8,128)(2,1)S(1)} %collective-permute-done.14.refs_3_, bf16[227,128]{1,0:T(8,128)(2,1)S(1)} %collective-permute-done.15.refs_4_, ...), custom_call_target="tpu_custom_call" | custom-call | flops 5000000000 | bytes 5000000 | tf_op jit(solution)/shard_map/pallas_call | solution.py:107
  149.4 3.0 %shard_map.264 = (f32[227,512]{1,0:T(8,128)}, f32[512,512]{1,0:T(8,128)}, f32[512,512]{1,0:T(8,128)}, f32[512,512]{1,0:T(8,128)}, f32[256,512]{1,0:T(8,128)}, /*...) custom-call(s32[1]{0:T(128)} %bitcast.2.refs_0_, ...), custom_call_target="tpu_custom_call" | custom-call | flops 4000000000 | bytes 4000000 | tf_op jit(solution)/shard_map/pallas_call | solution.py:107
  (57 shorter events, 0.1 us)
Async XLA Ops:
  0.6 1.2 copy-start
  1.8 0.7 copy-start.17
  2.5 8.7 %copy-start.1 = (bf16[2048,227]{0,1:T(8,128)(2,1)S(1)}, bf16[2048,227]{0,1:T(8,128)(2,1)}, u32[]{:S(2)}) copy-start(bf16[2048,227]{0,1:T(8,128)(2,1)} %param.18) | copy-start | bytes 2789380
  2.5 8.7 %copy-start.2 = (bf16[512,512]{1,0:T(8,128)(2,1)S(1)}, bf16[512,512]{1,0:T(8,128)(2,1)}, u32[]{:S(2)}) copy-start(bf16[512,512]{1,0:T(8,128)(2,1)} %refs_21_.1) | copy-start | bytes 1572868
  2.5 8.7 %copy-start.3 = (bf16[512,512]{1,0:T(8,128)(2,1)S(1)}, bf16[512,512]{1,0:T(8,128)(2,1)}, u32[]{:S(2)}) copy-start(bf16[512,512]{1,0:T(8,128)(2,1)} %refs_17_.3) | copy-start | bytes 1572868
  2.5 8.7 %copy-start.11 = (bf16[256,512]{1,0:T(8,128)(2,1)S(1)}, bf16[256,512]{1,0:T(8,128)(2,1)}, u32[]{:S(2)}) copy-start(bf16[256,512]{1,0:T(8,128)(2,1)} %refs_18_.1) | copy-start | bytes 786436
  2.5 8.7 %copy-start.12 = (bf16[227,512]{1,0:T(8,128)(2,1)S(1)}, bf16[227,512]{1,0:T(8,128)(2,1)}, u32[]{:S(2)}) copy-start(bf16[227,512]{1,0:T(8,128)(2,1)} %refs_20_.1) | copy-start | bytes 697348
  2.6 8.7 %copy-start.13 = (s32[1,4096]{1,0:T(1,128)S(1)}, s32[1,4096]{1,0:T(1,128)}, u32[]{:S(2)}) copy-start(s32[1,4096]{1,0:T(1,128)} %refs_2_.7) | copy-start | bytes 49156
  2.6 8.7 %copy-start.14 = (s32[1,4096]{1,0:T(1,128)S(1)}, s32[1,4096]{1,0:T(1,128)}, u32[]{:S(2)}) copy-start(s32[1,4096]{1,0:T(1,128)} %refs_3_.1) | copy-start | bytes 49156
  2.6 8.7 %copy-start.18 = (s32[1,2048]{1,0:T(1,128)S(1)}, s32[1,2048]{1,0:T(1,128)}, u32[]{:S(2)}) copy-start(s32[1,2048]{1,0:T(1,128)} %refs_1_.7) | copy-start | bytes 24580
  3.3 15.3 %collective-permute-start = (bf16[227,128]{1,0:T(8,128)(2,1)S(1)}, bf16[227,128]{1,0:T(8,128)(2,1)S(1)}, u32[]{:S(2)}, u32[]{:S(2)}) collective-permute-start(bf16[227,128]{1,0:T(8,128)(2,1)S(1)} %get-tuple-element.68.refs_10_), channel_id=1, source_target_pairs={{0,16},{16,32},{32,48},{48,64},{64,80},{80,96},{96,112},{112,0},{1... | collective-permute-start | bytes 174344 | tf_op jit(solution)/shard_map/ppermute | solution.py:443
  6.3 12.3 %collective-permute-start.1 = (bf16[227,128]{1,0:T(8,128)(2,1)S(1)}, bf16[227,128]{1,0:T(8,128)(2,1)S(1)}, u32[]{:S(2)}, u32[]{:S(2)}) collective-permute-start(bf16[227,128]{1,0:T(8,128)(2,1)S(1)} %get-tuple-element.69.refs_9_), channel_id=1, source_target_pairs={{16,0},{32,16},{48,32},{64,48},{80,64},{96,80},{112,96},{0,112},{1... | collective-permute-start | bytes 174344 | tf_op jit(solution)/shard_map/ppermute | solution.py:444
  6.3 12.3 %collective-permute-start.2 = (bf16[227,128]{1,0:T(8,128)(2,1)S(1)}, bf16[227,128]{1,0:T(8,128)(2,1)S(1)}, u32[]{:S(2)}, u32[]{:S(2)}) collective-permute-start(bf16[227,128]{1,0:T(8,128)(2,1)S(1)} %get-tuple-element.70), channel_id=1, source_target_pairs={{0,1},{1,2},{2,3},{3,4},{4,5},{5,6},{6,7},{7,8},{8,9},{9,10},{10,1... | collective-permute-start | bytes 174344 | tf_op jit(solution)/shard_map/ppermute | solution.py:445
  7.5 11.1 %collective-permute-start.3 = (bf16[227,128]{1,0:T(8,128)(2,1)S(1)}, bf16[227,128]{1,0:T(8,128)(2,1)S(1)}, u32[]{:S(2)}, u32[]{:S(2)}) collective-permute-start(bf16[227,128]{1,0:T(8,128)(2,1)S(1)} %get-tuple-element.71), channel_id=1, source_target_pairs={{1,0},{2,1},{3,2},{4,3},{5,4},{6,5},{7,6},{8,7},{9,8},{10,9},{11,1... | collective-permute-start | bytes 174344 | tf_op jit(solution)/shard_map/ppermute | solution.py:446
  11.3 7.3 %copy-start.4 = (bf16[512,512]{1,0:T(8,128)(2,1)S(1)}, bf16[512,512]{1,0:T(8,128)(2,1)}, u32[]{:S(2)}) copy-start(bf16[512,512]{1,0:T(8,128)(2,1)} %refs_12_.5) | copy-start | bytes 1572868
  11.3 7.3 %copy-start.19 = (s32[1,2,2,32]{3,2,1,0:T(2,128)S(1)}, s32[1,2,2,32]{3,2,1,0:T(2,128)}, u32[]{:S(2)}) copy-start(s32[1,2,2,32]{3,2,1,0:T(2,128)} %refs_5_.3) | copy-start | bytes 1540
  18.7 18.6 %copy-start.5 = (bf16[256,512]{1,0:T(8,128)(2,1)S(1)}, bf16[256,512]{1,0:T(8,128)(2,1)}, u32[]{:S(2)}) copy-start(bf16[256,512]{1,0:T(8,128)(2,1)} %refs_9_.1) | copy-start | bytes 786436
  18.7 18.6 %copy-start.6 = (bf16[256,512]{1,0:T(8,128)(2,1)S(1)}, bf16[256,512]{1,0:T(8,128)(2,1)}, u32[]{:S(2)}) copy-start(bf16[256,512]{1,0:T(8,128)(2,1)} %refs_10_.1) | copy-start | bytes 786436
  18.7 18.6 %copy-start.7 = (bf16[512,256]{1,0:T(8,128)(2,1)S(1)}, bf16[512,256]{1,0:T(8,128)(2,1)}, u32[]{:S(2)}) copy-start(bf16[512,256]{1,0:T(8,128)(2,1)} %refs_11_.3) | copy-start | bytes 786436
  18.7 18.6 %copy-start.8 = (bf16[256,512]{1,0:T(8,128)(2,1)S(1)}, bf16[256,512]{1,0:T(8,128)(2,1)}, u32[]{:S(2)}) copy-start(bf16[256,512]{1,0:T(8,128)(2,1)} %refs_12_.4) | copy-start | bytes 786436
  18.7 18.6 %copy-start.9 = (bf16[512,256]{1,0:T(8,128)(2,1)S(1)}, bf16[512,256]{1,0:T(8,128)(2,1)}, u32[]{:S(2)}) copy-start(bf16[512,256]{1,0:T(8,128)(2,1)} %refs_13_.1) | copy-start | bytes 786436
  18.7 18.6 %copy-start.10 = (bf16[256,512]{1,0:T(8,128)(2,1)S(1)}, bf16[256,512]{1,0:T(8,128)(2,1)}, u32[]{:S(2)}) copy-start(bf16[256,512]{1,0:T(8,128)(2,1)} %refs_8_.1) | copy-start | bytes 786436
  18.7 18.6 %copy-start.15 = (s32[1,2048]{1,0:T(1,128)S(1)}, s32[1,2048]{1,0:T(1,128)}, u32[]{:S(2)}) copy-start(s32[1,2048]{1,0:T(1,128)} %refs_1_.6) | copy-start | bytes 24580
  18.8 18.6 %copy-start.16 = (s32[1,2048]{1,0:T(1,128)S(1)}, s32[1,2048]{1,0:T(1,128)}, u32[]{:S(2)}) copy-start(s32[1,2048]{1,0:T(1,128)} %refs_2_.6) | copy-start | bytes 24580
  28.9 7.2 %collective-permute-start.4 = (bf16[32,256]{1,0:T(8,128)(2,1)S(1)}, bf16[32,256]{1,0:T(8,128)(2,1)S(1)}, u32[]{:S(2)}, u32[]{:S(2)}) collective-permute-start(bf16[32,256]{1,0:T(8,128)(2,1)S(1)} %get-tuple-element.76), channel_id=1, source_target_pairs={{0,16},{16,32},{32,48},{48,64},{64,80},{80,96},{96,112},{112,0},{1... | collective-permute-start | bytes 49160 | tf_op jit(solution)/shard_map/ppermute | solution.py:443
  31.1 5.1 %collective-permute-start.5 = (bf16[32,256]{1,0:T(8,128)(2,1)S(1)}, bf16[32,256]{1,0:T(8,128)(2,1)S(1)}, u32[]{:S(2)}, u32[]{:S(2)}) collective-permute-start(bf16[32,256]{1,0:T(8,128)(2,1)S(1)} %get-tuple-element.77), channel_id=1, source_target_pairs={{16,0},{32,16},{48,32},{64,48},{80,64},{96,80},{112,96},{0,112},{1... | collective-permute-start | bytes 49160 | tf_op jit(solution)/shard_map/ppermute | solution.py:444
  31.4 5.9 %collective-permute-start.6 = (bf16[32,256]{1,0:T(8,128)(2,1)S(1)}, bf16[32,256]{1,0:T(8,128)(2,1)S(1)}, u32[]{:S(2)}, u32[]{:S(2)}) collective-permute-start(bf16[32,256]{1,0:T(8,128)(2,1)S(1)} %get-tuple-element.78), channel_id=1, source_target_pairs={{0,1},{1,2},{2,3},{3,4},{4,5},{5,6},{6,7},{7,8},{8,9},{9,10},{10,1... | collective-permute-start | bytes 49160 | tf_op jit(solution)/shard_map/ppermute | solution.py:445
  31.4 5.9 %collective-permute-start.7 = (bf16[32,256]{1,0:T(8,128)(2,1)S(1)}, bf16[32,256]{1,0:T(8,128)(2,1)S(1)}, u32[]{:S(2)}, u32[]{:S(2)}) collective-permute-start(bf16[32,256]{1,0:T(8,128)(2,1)S(1)} %get-tuple-element.79), channel_id=1, source_target_pairs={{1,0},{2,1},{3,2},{4,3},{5,4},{6,5},{7,6},{8,7},{9,8},{10,9},{11,1... | collective-permute-start | bytes 49160 | tf_op jit(solution)/shard_map/ppermute | solution.py:446
  44.1 13.4 %collective-permute-start.10 = (bf16[32,256]{1,0:T(8,128)(2,1)S(1)}, bf16[32,256]{1,0:T(8,128)(2,1)S(1)}, u32[]{:S(2)}, u32[]{:S(2)}) collective-permute-start(bf16[32,256]{1,0:T(8,128)(2,1)S(1)} %get-tuple-element.82), channel_id=1, source_target_pairs={{0,1},{1,2},{2,3},{3,4},{4,5},{5,6},{6,7},{7,8},{8,9},{9,10},{10,1... | collective-permute-start | bytes 49160 | tf_op jit(solution)/shard_map/ppermute | solution.py:445
  44.2 13.3 %collective-permute-start.11 = (bf16[32,256]{1,0:T(8,128)(2,1)S(1)}, bf16[32,256]{1,0:T(8,128)(2,1)S(1)}, u32[]{:S(2)}, u32[]{:S(2)}) collective-permute-start(bf16[32,256]{1,0:T(8,128)(2,1)S(1)} %get-tuple-element.83), channel_id=1, source_target_pairs={{1,0},{2,1},{3,2},{4,3},{5,4},{6,5},{7,6},{8,7},{9,8},{10,9},{11,1... | collective-permute-start | bytes 49160 | tf_op jit(solution)/shard_map/ppermute | solution.py:446
  49.0 8.5 %collective-permute-start.8 = (bf16[32,256]{1,0:T(8,128)(2,1)S(1)}, bf16[32,256]{1,0:T(8,128)(2,1)S(1)}, u32[]{:S(2)}, u32[]{:S(2)}) collective-permute-start(bf16[32,256]{1,0:T(8,128)(2,1)S(1)} %get-tuple-element.80), channel_id=1, source_target_pairs={{0,16},{16,32},{32,48},{48,64},{64,80},{80,96},{96,112},{112,0},{1... | collective-permute-start | bytes 49160 | tf_op jit(solution)/shard_map/ppermute | solution.py:443
  52.2 5.3 %collective-permute-start.9 = (bf16[32,256]{1,0:T(8,128)(2,1)S(1)}, bf16[32,256]{1,0:T(8,128)(2,1)S(1)}, u32[]{:S(2)}, u32[]{:S(2)}) collective-permute-start(bf16[32,256]{1,0:T(8,128)(2,1)S(1)} %get-tuple-element.81), channel_id=1, source_target_pairs={{16,0},{32,16},{48,32},{64,48},{80,64},{96,80},{112,96},{0,112},{1... | collective-permute-start | bytes 49160 | tf_op jit(solution)/shard_map/ppermute | solution.py:444
  54.5 19.0 %collective-permute-start.12 = (bf16[640,512]{1,0:T(8,128)(2,1)S(1)}, bf16[640,512]{1,0:T(8,128)(2,1)S(1)}, u32[]{:S(2)}, u32[]{:S(2)}) collective-permute-start(bf16[640,512]{1,0:T(8,128)(2,1)S(1)} %get-tuple-element.101), channel_id=1, source_target_pairs={{0,16},{16,0},{1,17},{17,1},{2,18},{18,2},{3,19},{19,3},{4,20},{20... | collective-permute-start | bytes 1966088 | tf_op jit(solution)/shard_map/ppermute | solution.py:451
  72.4 6.4 %copy-start.20 = (bf16[227,1536]{1,0:T(8,128)(2,1)}, bf16[227,1536]{1,0:T(8,128)(2,1)S(1)}, u32[]{:S(2)}) copy-start(bf16[227,1536]{1,0:T(8,128)(2,1)S(1)} %get-tuple-element.99.refs_2_) | copy-start | bytes 2092036
  72.4 6.1 %collective-permute-start.13 = (bf16[896,512]{1,0:T(8,128)(2,1)S(1)}, bf16[896,512]{1,0:T(8,128)(2,1)S(1)}, u32[]{:S(2)}, u32[]{:S(2)}) collective-permute-start(bf16[896,512]{1,0:T(8,128)(2,1)S(1)} %get-tuple-element.103), channel_id=1, source_target_pairs={{0,16},{16,0},{1,17},{17,1},{2,18},{18,2},{3,19},{19,3},{4,20},{20... | collective-permute-start | bytes 2752520 | tf_op jit(solution)/shard_map/ppermute | solution.py:451
  73.0 5.9 %collective-permute-start.14 = (bf16[227,128]{1,0:T(8,128)(2,1)S(1)}, bf16[227,128]{1,0:T(8,128)(2,1)S(1)}, u32[]{:S(2)}, u32[]{:S(2)}) collective-permute-start(bf16[227,128]{1,0:T(8,128)(2,1)S(1)} %get-tuple-element.104.refs_8_), channel_id=1, source_target_pairs={{0,16},{16,32},{32,48},{48,64},{64,80},{80,96},{96,112},{112,0},{1... | collective-permute-start | bytes 174344 | tf_op jit(solution)/shard_map/ppermute | solution.py:443
  73.0 5.9 %collective-permute-start.15 = (bf16[227,128]{1,0:T(8,128)(2,1)S(1)}, bf16[227,128]{1,0:T(8,128)(2,1)S(1)}, u32[]{:S(2)}, u32[]{:S(2)}) collective-permute-start(bf16[227,128]{1,0:T(8,128)(2,1)S(1)} %get-tuple-element.105.refs_7_), channel_id=1, source_target_pairs={{16,0},{32,16},{48,32},{64,48},{80,64},{96,80},{112,96},{0,112},{1... | collective-permute-start | bytes 174344 | tf_op jit(solution)/shard_map/ppermute | solution.py:444
  73.5 6.4 %collective-permute-start.16 = (bf16[227,128]{1,0:T(8,128)(2,1)S(1)}, bf16[227,128]{1,0:T(8,128)(2,1)S(1)}, u32[]{:S(2)}, u32[]{:S(2)}) collective-permute-start(bf16[227,128]{1,0:T(8,128)(2,1)S(1)} %get-tuple-element.106), channel_id=1, source_target_pairs={{0,1},{1,2},{2,3},{3,4},{4,5},{5,6},{6,7},{7,8},{8,9},{9,10},{10,1... | collective-permute-start | bytes 174344 | tf_op jit(solution)/shard_map/ppermute | solution.py:445
  73.5 6.4 %collective-permute-start.17 = (bf16[227,128]{1,0:T(8,128)(2,1)S(1)}, bf16[227,128]{1,0:T(8,128)(2,1)S(1)}, u32[]{:S(2)}, u32[]{:S(2)}) collective-permute-start(bf16[227,128]{1,0:T(8,128)(2,1)S(1)} %get-tuple-element.107), channel_id=1, source_target_pairs={{1,0},{2,1},{3,2},{4,3},{5,4},{6,5},{7,6},{8,7},{9,8},{10,9},{11,1... | collective-permute-start | bytes 174344 | tf_op jit(solution)/shard_map/ppermute | solution.py:446
  104.8 9.8 %collective-permute-start.18 = (bf16[96,512]{1,0:T(8,128)(2,1)S(1)}, bf16[96,512]{1,0:T(8,128)(2,1)S(1)}, u32[]{:S(2)}, u32[]{:S(2)}) collective-permute-start(bf16[96,512]{1,0:T(8,128)(2,1)S(1)} %reduce_sum.12), channel_id=1, source_target_pairs={{0,64},{32,96},{64,0},{96,32},{1,65},{33,97},{65,1},{97,33},{2,66}... | collective-permute-start | bytes 294920 | tf_op jit(solution)/shard_map/ppermute | solution.py:540
  111.9 5.2 %collective-permute-start.19 = (bf16[96,512]{1,0:T(8,128)(2,1)S(1)}, bf16[96,512]{1,0:T(8,128)(2,1)S(1)}, u32[]{:S(2)}, u32[]{:S(2)}) collective-permute-start(bf16[96,512]{1,0:T(8,128)(2,1)S(1)} %reduce_sum.12), channel_id=1, source_target_pairs={{0,32},{32,64},{64,96},{96,0},{1,33},{33,65},{65,97},{97,1},{2,34}... | collective-permute-start | bytes 294920 | tf_op jit(solution)/shard_map/ppermute | solution.py:540
  111.9 5.2 %collective-permute-start.20 = (bf16[96,512]{1,0:T(8,128)(2,1)S(1)}, bf16[96,512]{1,0:T(8,128)(2,1)S(1)}, u32[]{:S(2)}, u32[]{:S(2)}) collective-permute-start(bf16[96,512]{1,0:T(8,128)(2,1)S(1)} %reduce_sum.12), channel_id=1, source_target_pairs={{0,96},{32,0},{64,32},{96,64},{1,97},{33,1},{65,33},{97,65},{2,98}... | collective-permute-start | bytes 294920 | tf_op jit(solution)/shard_map/ppermute | solution.py:540
  117.3 27.5 %copy-start.21 = (bf16[227,1536]{1,0:T(8,128)(2,1)S(1)}, bf16[227,1536]{1,0:T(8,128)(2,1)}, u32[]{:S(2)}) copy-start(bf16[227,1536]{1,0:T(8,128)(2,1)} %copy-done.20) | copy-start | bytes 2092036
  141.6 7.7 %collective-permute-start.21 = (bf16[1536,512]{1,0:T(8,128)(2,1)S(1)}, bf16[1536,512]{1,0:T(8,128)(2,1)S(1)}, u32[]{:S(2)}, u32[]{:S(2)}) collective-permute-start(bf16[1536,512]{1,0:T(8,128)(2,1)S(1)} %bitcast.7), channel_id=1, source_target_pairs={{0,16},{16,0},{1,17},{17,1},{2,18},{18,2},{3,19},{19,3},{4,20},{20... | collective-permute-start | bytes 4718600 | tf_op jit(solution)/shard_map/ppermute | solution.py:451
where the time goes:
time: 153 us
  blocking collectives  49 us (32%)
  Pallas kernels  48 us (31%)
  starting transfers between devices  46.6 us (30%)
  waiting for transfers between devices  4.62 us (3%)
  local copies, waits for them, and re-layouts  2.13 us (1%)
    pallas_call x8, Pallas kernels, call(): pl.pallas_call(run, out_shape=outs, in_specs=[pl.BlockSpec(memory_space=s...  48 us
    all_to_all x1, blocking collectives, body(): parts = lax.all_to_all(pair, PATCH, 0, 0)  24.7 us
    all_to_all x1, blocking collectives, body(): lax.all_to_all(jnp.broadcast_to(total[None], parts.shape), PATCH, 0, 0)  24.3 us
    ppermute x4, starting transfers between devices, trade(): lax.ppermute(west, PATCH, left)  18.1 us
    ppermute x3, starting transfers between devices, body(): lax.ppermute(part, 'z', [(i, (i + k) % 4) for i in range(4)])  9.82 us
    ppermute x4, starting transfers between devices, trade(): lax.ppermute(above, BAND, up)  8.41 us
    ppermute x3, starting transfers between devices, swap_cores(): return lax.ppermute(value, 'core', [(0, 1), (1, 0)])  6.78 us
  transfers between devices with their start and end apart: 22, of which 3 were waited for; matrix products, arithmetic and copies ran while one was open for 0% of the time, Pallas kernels for 18%

commit v1 on v0

--- a/solution.py
+++ b/solution.py
@@ -13,6 +13,7 @@
 LANES = 128
 EDGE_TILE = 1024
 ROW_TILE = 512
+BACK_TILE = 1024
 VMEM_LIMIT = 32 * 1024 * 1024
 PIECES = 4
 BAND = ("z", "core")
@@ -162,19 +163,20 @@
 
 def encode_kernel(
     flag_ref, src_ref, dst_ref, row_ref, halo_ref, in0, in1, in2, in3, own0, own1, embed_ref, send_ref,
-    sender_ref, node_ref, column_ref, out_w_ref, mesh_ref,
-    rim_ref, slope0, slope1, gathered_ref, latent_ref, h00, h01, h10, h11,
+    keep_rows_ref, sender_ref, node_ref, column_ref, out_w_ref, mesh_ref,
+    rows_ref, slope0, slope1, gathered_ref, latent_ref, h00, h01, h10, h11,
     table, total,
 ):
     keep = sender_ref.shape[0]
     rim = in0.shape[1]
     rows = keep + 4 * rim
     nodes = node_ref.shape[0]
-    rim_ref[:, 0:rim] = jnp.where(flag_ref[0] > 0, in0[...], own0[...])
-    rim_ref[:, rim : 2 * rim] = jnp.where(flag_ref[1] > 0, in1[...], own1[...])
-    rim_ref[:, 2 * rim : 3 * rim] = in2[...]
-    rim_ref[:, 3 * rim : 4 * rim] = in3[...]
-    embedded = silu_both(mm_left(rim_ref[...], embed_ref[...]))[0].astype(BF16)
+    rows_ref[:, 0:keep] = keep_rows_ref[...]
+    rows_ref[:, keep : keep + rim] = jnp.where(flag_ref[0] > 0, in0[...], own0[...])
+    rows_ref[:, keep + rim : keep + 2 * rim] = jnp.where(flag_ref[1] > 0, in1[...], own1[...])
+    rows_ref[:, keep + 2 * rim : keep + 3 * rim] = in2[...]
+    rows_ref[:, keep + 3 * rim : rows] = in3[...]
+    embedded = silu_both(mm_left(rows_ref[:, keep:], embed_ref[...]))[0].astype(BF16)
     table[keep:rows, :] = mm(embedded, send_ref[...]).astype(BF16)
     table[0:keep, :] = sender_ref[...]
     table[rows : rows + nodes, :] = node_ref[...]
@@ -309,12 +311,11 @@
 
 def encoder_back_kernel(
     core_ref, flag_ref, src_ref, dst_ref, row_ref, halo_ref, r0, r1, r2, r3, lower_grad_ref, coupled_grad_ref, out_w_ref,
-    column_ref, slope0, slope1, gathered_ref, recv_ref, mesh_ref, rim_rows_ref, embed_ref, send_ref, keep_rows_ref,
-    keep_grad_ref, g0, g1, g2, g3, mesh_grad_ref, mine_ref, other_ref,
+    column_ref, slope0, slope1, gathered_ref, recv_ref, mesh_ref, embed_ref, send_ref, rows_ref,
+    rows_grad_ref, g0, g1, g2, g3, mesh_grad_ref, mine_ref, other_ref,
     edge_s, latent_s, nodes_s, sum_send, sum_embed,
 ):
     nodes, dim = mesh_ref.shape
-    keep = keep_rows_ref.shape[1]
     rim = g0.shape[1]
     lower_grad = lower_grad_ref[...]
     for a, b, ref in ((0, 0, r0), (0, 1, r1), (1, 0, r2), (1, 1, r3)):
@@ -348,41 +349,37 @@
     mesh_grad_ref.send()
     extra = src_ref[:, rows:]
 
-    def back(cols, start, count):
-        ids = lax.broadcasted_iota(jnp.int32, (count, extra.shape[1]), 0) + start
+    sum_send[...] = jnp.zeros_like(sum_send)
+    sum_embed[...] = jnp.zeros_like(sum_embed)
+
+    def back(start):
+        here = pl.ds(start, BACK_TILE)
+        cols = rows_ref[:, here]
+        ids = lax.broadcasted_iota(jnp.int32, (BACK_TILE, extra.shape[1]), 0) + start
         table = jnp.where(ids == extra, 1.0, 0.0).astype(BF16)
-        own = edge_s[pl.ds(start, count), :].astype(F32)
+        own = edge_s[here, :].astype(F32)
         sender_grad = (own + mm(table, edge_s[rows:, :])).astype(BF16)
         act, slope = silu_both(mm_left(cols, embed_ref[...]))
         embedded_grad = mm_right(sender_grad, send_ref[...]).astype(BF16)
         embed_grad = (embedded_grad.astype(F32) * slope).astype(BF16)
-        cols_grad = mm_right(embed_ref[...], embed_grad).astype(BF16)
-        return cols_grad, mm_left(act.astype(BF16), sender_grad), mm(cols, embed_grad)
-
-    rim_grad, send_part, embed_part = back(rim_rows_ref[...], keep, 4 * rim)
-    sum_send[...] = send_part
-    sum_embed[...] = embed_part
+        rows_grad_ref[:, here] = mm_right(embed_ref[...], embed_grad).astype(BF16)
+        sum_send[...] += mm_left(act.astype(BF16), sender_grad)
+        sum_embed[...] += mm(cols, embed_grad)
+
+    tiles(rows, BACK_TILE, back)
     for k, ref in enumerate((g0, g1, g2, g3)):
-        ref[...] = rim_grad[:, k * rim : (k + 1) * rim]
-
-    def kept(start):
-        here = pl.ds(start, ROW_TILE)
-        cols_grad, send_part, embed_part = back(keep_rows_ref[:, here], start, ROW_TILE)
-        keep_grad_ref[:, here] = cols_grad
-        sum_send[...] += send_part
-        sum_embed[...] += embed_part
-
-    tiles(keep, ROW_TILE, kept)
+        start = rows - (4 - k) * rim
+        ref[...] = rows_grad_ref[:, start : start + rim]
     store_halves(core_ref, mine_ref, other_ref, 2 * dim, sum_send[...])
     grad_embed = sum_embed[...]
     pad = jnp.zeros((half - grad_embed.shape[0], dim), F32)
     store_halves(core_ref, mine_ref, other_ref, 3 * dim, jnp.concatenate([grad_embed, pad], axis=0))
 
 
-def place_kernel(flag_ref, order_ref, keep_ref, in0, in1, in2, in3, own0, own1, grid_grad_ref, all_s):
-    keep = keep_ref.shape[1]
+def place_kernel(flag_ref, order_ref, rows_ref, in0, in1, in2, in3, own0, own1, grid_grad_ref, all_s):
     rim = in0.shape[1]
-    all_s[:, 0:keep] = keep_ref[...]
+    keep = rows_ref.shape[1] - 4 * rim
+    all_s[:, 0:keep] = rows_ref[:, 0:keep]
     all_s[:, keep : keep + rim] = jnp.where(flag_ref[0] > 0, in0[...], own0[...])
     all_s[:, keep + rim : keep + 2 * rim] = jnp.where(flag_ref[1] > 0, in1[...], own1[...])
     all_s[:, keep + 2 * rim : keep + 3 * rim] = in2[...]
@@ -481,14 +478,14 @@
     )
 
     outs = [
-        shape((chans, 4 * rim), BF16), shape((grid_rows, dim), BF16), shape((edges - grid_rows, dim), BF16),
+        shape((chans, grid_rows), BF16), shape((grid_rows, dim), BF16), shape((edges - grid_rows, dim), BF16),
         shape((nodes, dim), BF16), shape((nodes, dim), BF16),
     ] + [shape((width, half), BF16)] * 4
     ins = (
         flags, enc_src, enc_dst, row, halo_send, *arrived, own[0], own[1], w_embed, w_send,
-        keep_sender, node_part, column, w_out, mesh_feats,
-    )
-    rim_rows, slope0, slope1, gathered, latent, h00, h01, h10, h11 = call(
+        keep_rows, keep_sender, node_part, column, w_out, mesh_feats,
+    )
+    all_rows, slope0, slope1, gathered, latent, h00, h01, h10, h11 = call(
         encode_kernel, outs, 12, ins, scalars=1,
         scratch=[pltpu.VMEM((grid_rows + nodes, dim), BF16), pltpu.VMEM((nodes, dim), F32)],
     )
@@ -515,13 +512,13 @@
     lower_grad, a_mine = lax.optimization_barrier((lower_grad, a_mine))
 
     b_rows = 3 * dim + half
-    outs = [shape((chans, keep), BF16)] + [shape((chans, rim), BF16)] * 4 + [shape((nodes, dim), F32)]
+    outs = [shape((chans, grid_rows), BF16)] + [shape((chans, rim), BF16)] * 4 + [shape((nodes, dim), F32)]
     outs += [shape((b_rows // 2, dim), BF16)] * 2
     ins = (
         core, flags, enc_src, enc_dst, row, halo_send, *returned, lower_grad, coupled_grad, w_out,
-        column, slope0, slope1, gathered, w_recv, mesh_feats, rim_rows, w_embed, w_send, keep_rows,
-    )
-    keep_grad, q0, q1, q2, q3, mesh_grad, b_mine, b_other = call(
+        column, slope0, slope1, gathered, w_recv, mesh_feats, w_embed, w_send, all_rows,
+    )
+    rows_grad, q0, q1, q2, q3, mesh_grad, b_mine, b_other = call(
         encoder_back_kernel, outs, 14, ins, scalars=2, sent=(5,),
         scratch=[
             pltpu.VMEM((edges, dim), BF16), pltpu.VMEM((nodes, dim), BF16), pltpu.VMEM((nodes, dim), F32),
@@ -534,18 +531,19 @@
     packed = (a_rows + b_rows) // 2
     pair = jnp.concatenate([a_mine.astype(F32) + a_in.astype(F32), b_mine.astype(F32) + b_in.astype(F32)], axis=0)
     pair = pair.astype(BF16).reshape(patches, packed // patches, dim)
-    pair, *back = lax.optimization_barrier((pair, *back))
     parts = lax.all_to_all(pair, PATCH, 0, 0)
     part = jnp.sum(parts.astype(F32), axis=0).astype(BF16)
+    part, *back = lax.optimization_barrier((part, *back))
+    ins = (flags, send_rows, rows_grad, *back, q0, q1)
+    (grid_grad,) = call(
+        place_kernel, [shape((chans, grid_rows), BF16)], 5, ins, scalars=1, scratch=[pltpu.VMEM((chans, grid_rows), BF16)]
+    )
     away = [part] + [lax.ppermute(part, "z", [(i, (i + k) % 4) for i in range(4)]) for k in (1, 2, 3)]
     away = [piece.astype(F32) for piece in away]
     total = ((away[0] + away[2]) + (away[1] + away[3])).astype(BF16)
     mine = lax.all_to_all(jnp.broadcast_to(total[None], parts.shape), PATCH, 0, 0).reshape(packed, dim)
+    mine, grid_grad = lax.optimization_barrier((mine, grid_grad))
     other = swap_cores(mine)
-    ins = (flags, send_rows, keep_grad, *back, q0, q1)
-    (grid_grad,) = call(
-        place_kernel, [shape((chans, grid_rows), BF16)], 5, ins, scalars=1, scratch=[pltpu.VMEM((chans, grid_rows), BF16)]
-    )
     outs = [shape((chans, dim), F32)] + [shape((dim, dim), F32)] * 3 + [shape((half, dim), F32)] * 2
     outs += [shape((dim, half), F32), shape((half, dim), F32), shape((dim, half), F32)]
     totals = call(functools.partial(unpack_kernel, a_rows), outs, 4, (core, mine, other), scalars=1, sent=tuple(range(9)))

time: 153 us -> 151 us (0.987)
  blocking collectives: 49 us -> 0 us
  waiting for transfers between devices: 4.62 us -> 44.1 us
  starting transfers between devices: 46.6 us -> 49.8 us
  other arithmetic: 0.92 us -> 3.47 us
  local copies, waits for them, and re-layouts: 2.13 us -> 4.49 us
    all_to_all x2 -> x0, blocking collectives: 49 us -> none  [the longest x1 24.7 us: body(): parts = lax.all_to_all(pair, PATCH, 0, 0)]
    all_to_all x0 -> x2, waiting for transfers between devices: none -> 35 us  [the longest x1 20 us: body(): parts = lax.all_to_all(pair, PATCH, 0, 0)]
    all_to_all x0 -> x2, starting transfers between devices: none -> 9.41 us  [the longest x1 5.02 us: body(): lax.all_to_all(jnp.broadcast_to(total[None], parts.shape), PATCH, 0, 0)]
    ppermute x3, starting transfers between devices: 9.82 us -> 2.82 us  [body(): lax.ppermute(part, 'z', [(i, (i + k) % 4) for i in range(4)])]
    ppermute x3, waiting for transfers between devices: 0.01 us -> 4.95 us  [swap_cores(): return lax.ppermute(value, 'core', [(0, 1), (1, 0)])]
    ppermute x4, starting transfers between devices: 8.41 us -> 5.23 us  [trade(): lax.ppermute(above, BAND, up)]
    ppermute x4, starting transfers between devices: 2.21 us -> 4.86 us  [trade(): lax.ppermute(below, BAND, down)]
  transfers between devices with their start and end apart: 22 -> 24, of which waited for: 3 -> 7; matrix products, arithmetic and copies ran while one was open for 0% -> 1% of each run, Pallas kernels for 18% -> 18%
where the time goes in v1:
time: 151 us
  starting transfers between devices  49.8 us (33%)
  Pallas kernels  47.8 us (32%)
  waiting for transfers between devices  44.1 us (29%)
  local copies, waits for them, and re-layouts  4.49 us (3%)
  other arithmetic  3.47 us (2%)
    pallas_call x8, Pallas kernels, call(): pl.pallas_call(run, out_shape=outs, in_specs=[pl.BlockSpec(memory_space=s...  47.8 us
    all_to_all x1, waiting for transfers between devices, body(): parts = lax.all_to_all(pair, PATCH, 0, 0)  20 us
    ppermute x4, starting transfers between devices, trade(): lax.ppermute(west, PATCH, left)  17 us
    all_to_all x1, waiting for transfers between devices, body(): lax.all_to_all(jnp.broadcast_to(total[None], parts.shape), PATCH, 0, 0)  15 us
    ppermute x3, starting transfers between devices, swap_cores(): return lax.ppermute(value, 'core', [(0, 1), (1, 0)])  7.87 us
    ppermute x4, starting transfers between devices, trade(): lax.ppermute(above, BAND, up)  5.23 us
    all_to_all x1, starting transfers between devices, body(): lax.all_to_all(jnp.broadcast_to(total[None], parts.shape), PATCH, 0, 0)  5.02 us
    ppermute x3, waiting for transfers between devices, swap_cores(): return lax.ppermute(value, 'core', [(0, 1), (1, 0)])  4.95 us
  transfers between devices with their start and end apart: 24, of which 7 were waited for; matrix products, arithmetic and copies ran while one was open for 1% of the time, Pallas kernels for 18%

profile of v1, /device:TPU:1, one launch (start us, length us, event | category | flops | bytes accessed | tf_op | source)
XLA Modules:
  0.0 150.9 jit_solution(8529655980850021821)
XLA Ops:
  0.7 1.2 copy-done
  1.8 0.7 copy-done.17
  2.6 0.7 shard_map.258
  3.3 3.0 %collective-permute-start = (bf16[227,128]{1,0:T(8,128)(2,1)S(1)}, bf16[227,128]{1,0:T(8,128)(2,1)S(1)}, u32[]{:S(2)}, u32[]{:S(2)}) collective-permute-start(bf16[227,128]{1,0:T(8,128)(2,1)S(1)} %get-tuple-element.70.refs_10_), channel_id=1, source_target_pairs={{0,16},{16,32},{32,48},{48,64},{64,80},{80,96},{96,112},{112,0},{1... | collective-permute-start | bytes 174344 | tf_op jit(solution)/shard_map/ppermute | solution.py:440
  6.3 1.2 collective-permute-start.2
  7.5 3.7 %collective-permute-start.3 = (bf16[227,128]{1,0:T(8,128)(2,1)S(1)}, bf16[227,128]{1,0:T(8,128)(2,1)S(1)}, u32[]{:S(2)}, u32[]{:S(2)}) collective-permute-start(bf16[227,128]{1,0:T(8,128)(2,1)S(1)} %get-tuple-element.73), channel_id=1, source_target_pairs={{1,0},{2,1},{3,2},{4,3},{5,4},{6,5},{7,6},{8,7},{9,8},{10,9},{11,1... | collective-permute-start | bytes 174344 | tf_op jit(solution)/shard_map/ppermute | solution.py:443
  11.3 7.2 %shard_map.257 = (bf16[227,1536]{1,0:T(8,128)(2,1)S(1)}, bf16[1536,512]{1,0:T(8,128)(2,1)S(1)}, bf16[256,512]{1,0:T(8,128)(2,1)S(1)}, bf16[2048,128]{1,0:T(8,128)(2,1)S(1)}, s32[1,2048]{1,0:T(1,128)S(1)}) custom-call(s32[1,2048]{1,0:T(1,128)S(1)} %copy-done.18, s32[1,4096]{1,0:T(1,128)S(1)} %copy-done.13, s32[1,4096]{1,0:T(1,128)S(1)} %copy-done.14, ...), custom_call_target="tpu_custom_call" | custom-call | flops 6000000000 | bytes 6000000 | tf_op jit(solution)/shard_map/pallas_call | solution.py:108
  18.5 0.1 pad_add_fusion.refs_0_.refs_1_
  18.7 0.0 copy-start.5
  18.7 0.0 copy-start.6
  18.7 0.0 copy-start.9
  18.8 10.2 %shard_map.259 = (bf16[227,2048]{1,0:T(8,128)(2,1)S(1)}, bf16[2048,512]{1,0:T(8,128)(2,1)S(1)}, bf16[2048,512]{1,0:T(8,128)(2,1)S(1)}, bf16[256,512]{1,0:T(8,128...) custom-call(s32[2]{0:T(128)S(1)} %pad_add_fusion.refs_0_.refs_1_, ...), custom_call_target="tpu_custom_call" | custom-call | flops 12000000000 | bytes 12000000 | tf_op jit(solution)/shard_map/pallas_call | solution.py:108
  29.0 2.2 %collective-permute-start.4 = (bf16[32,256]{1,0:T(8,128)(2,1)S(1)}, bf16[32,256]{1,0:T(8,128)(2,1)S(1)}, u32[]{:S(2)}, u32[]{:S(2)}) collective-permute-start(bf16[32,256]{1,0:T(8,128)(2,1)S(1)} %get-tuple-element.79), channel_id=1, source_target_pairs={{0,16},{16,32},{32,48},{48,64},{64,80},{80,96},{96,112},{112,0},{1... | collective-permute-start | bytes 49160 | tf_op jit(solution)/shard_map/ppermute | solution.py:440
  31.2 0.3 collective-permute-start.5
  31.4 4.8 %collective-permute-start.7 = (bf16[32,256]{1,0:T(8,128)(2,1)S(1)}, bf16[32,256]{1,0:T(8,128)(2,1)S(1)}, u32[]{:S(2)}, u32[]{:S(2)}) collective-permute-start(bf16[32,256]{1,0:T(8,128)(2,1)S(1)} %get-tuple-element.82), channel_id=1, source_target_pairs={{1,0},{2,1},{3,2},{4,3},{5,4},{6,5},{7,6},{8,7},{9,8},{10,9},{11,1... | collective-permute-start | bytes 49160 | tf_op jit(solution)/shard_map/ppermute | solution.py:443
  36.2 1.1 collective-permute-done.6.refs_7_
  37.4 6.7 %shard_map.260 = (bf16[32,256]{1,0:T(8,128)(2,1)S(1)}, bf16[32,256]{1,0:T(8,128)(2,1)S(1)}, bf16[32,256]{1,0:T(8,128)(2,1)S(1)}, bf16[32,256]{1,0:T(8,128)(2,1)S...) custom-call(s32[2]{0:T(128)S(1)} %pad_add_fusion.refs_0_.refs_1_, ...), custom_call_target="tpu_custom_call" | custom-call | flops 6000000000 | bytes 6000000 | tf_op jit(solution)/shard_map/pallas_call | solution.py:108
  44.2 4.1 %collective-permute-start.10 = (bf16[32,256]{1,0:T(8,128)(2,1)S(1)}, bf16[32,256]{1,0:T(8,128)(2,1)S(1)}, u32[]{:S(2)}, u32[]{:S(2)}) collective-permute-start(bf16[32,256]{1,0:T(8,128)(2,1)S(1)} %get-tuple-element.95), channel_id=1, source_target_pairs={{16,0},{32,16},{48,32},{64,48},{80,64},{96,80},{112,96},{0,112},{1... | collective-permute-start | bytes 49160 | tf_op jit(solution)/shard_map/ppermute | solution.py:441
  48.3 5.1 %collective-permute-start.12 = (bf16[32,256]{1,0:T(8,128)(2,1)S(1)}, bf16[32,256]{1,0:T(8,128)(2,1)S(1)}, u32[]{:S(2)}, u32[]{:S(2)}) collective-permute-start(bf16[32,256]{1,0:T(8,128)(2,1)S(1)} %get-tuple-element.97), channel_id=1, source_target_pairs={{1,0},{2,1},{3,2},{4,3},{5,4},{6,5},{7,6},{8,7},{9,8},{10,9},{11,1... | collective-permute-start | bytes 49160 | tf_op jit(solution)/shard_map/ppermute | solution.py:443
  53.3 0.8 shard_map.261
  54.1 0.6 collective-permute-start.8
  54.7 14.5 %shard_map.262 = (bf16[227,2048]{1,0:T(8,128)(2,1)S(1)}, bf16[227,128]{1,0:T(8,128)(2,1)S(1)}, bf16[227,128]{1,0:T(8,128)(2,1)S(1)}, bf16[227,128]{1,0:T(8,128)(...) custom-call(s32[1]{0:T(128)} %bitcast.3.refs_0_, ...), custom_call_target="tpu_custom_call" | custom-call | flops 14000000000 | bytes 14000000 | tf_op jit(solution)/shard_map/pallas_call | solution.py:108
  69.3 3.4 %collective-permute-start.13 = (bf16[896,512]{1,0:T(8,128)(2,1)S(1)}, bf16[896,512]{1,0:T(8,128)(2,1)S(1)}, u32[]{:S(2)}, u32[]{:S(2)}) collective-permute-start(bf16[896,512]{1,0:T(8,128)(2,1)S(1)} %get-tuple-element.104), channel_id=1, source_target_pairs={{0,16},{16,0},{1,17},{17,1},{2,18},{18,2},{3,19},{19,3},{4,20},{20... | collective-permute-start | bytes 2752520 | tf_op jit(solution)/shard_map/ppermute | solution.py:448
  72.7 0.2 add_convert_fusion.1
  72.9 1.9 %collective-permute-done.13 = bf16[896,512]{1,0:T(8,128)(2,1)S(1)} collective-permute-done((bf16[896,512]{1,0:T(8,128)(2,1)S(1)}, bf16[896,512]{1,0:T(8,128)(2,1)S(1)}, u32[]{:S(2)}, u32[]{:S(2)}) %collective-permute-start.13) | collective-permute-done | bytes 917536 | tf_op jit(solution)/shard_map/ppermute | solution.py:448
  74.8 0.3 add_convert_fusion
  75.1 1.2 pad_maximum_fusion
  76.3 4.4 %all-to-all-start = ((bf16[16,96,512]{2,1,0:T(8,128)(2,1)}), bf16[16,96,512]{2,1,0:T(8,128)(2,1)}, u32[]{:S(2)}, u32[]{:S(2)}) async-start(bf16[16,96,512]{2,1,0:T(8,128)(2,1)} %bitcast.4), calls=%async_computation | async-start | bytes 3145728 | tf_op jit(solution)/shard_map/all_to_all | solution.py:534
  80.7 0.0 collective-permute-start.14
  80.8 0.5 collective-permute-start.15
  81.3 1.3 collective-permute-start.16
  82.6 3.4 %collective-permute-start.17 = (bf16[227,128]{1,0:T(8,128)(2,1)S(1)}, bf16[227,128]{1,0:T(8,128)(2,1)S(1)}, u32[]{:S(2)}, u32[]{:S(2)}) collective-permute-start(bf16[227,128]{1,0:T(8,128)(2,1)S(1)} %get-tuple-element.108), channel_id=1, source_target_pairs={{1,0},{2,1},{3,2},{4,3},{5,4},{6,5},{7,6},{8,7},{9,8},{10,9},{11,1... | collective-permute-start | bytes 174344 | tf_op jit(solution)/shard_map/ppermute | solution.py:443
  86.1 20.0 %all-to-all-done = bf16[16,96,512]{2,1,0:T(8,128)(2,1)} async-done(((bf16[16,96,512]{2,1,0:T(8,128)(2,1)}), bf16[16,96,512]{2,1,0:T(8,128)(2,1)}, u32[]{:S(2)}, u32[]{:S(2)}) %all-to-all-start) | async-done | bytes 1572896 | tf_op jit(solution)/shard_map/all_to_all | solution.py:534
  106.1 1.6 %reduce_sum.12 = bf16[96,512]{1,0:T(8,128)(2,1)S(1)} reduce(bf16[16,96,512]{2,1,0:T(8,128)(2,1)} %all-to-all-done, bf16[]{:T(256)} %constant.18.clone.1), dimensions={0}, to_apply=%region_0.0 | reduce | flops 737280 | bytes 1671170 | tf_op jit(solution)/shard_map/reduce_sum | solution.py:535
  107.8 0.1 collective-permute-start.18
  107.8 0.1 collective-permute-start.19
  107.9 2.7 %collective-permute-start.20 = (bf16[96,512]{1,0:T(8,128)(2,1)S(1)}, bf16[96,512]{1,0:T(8,128)(2,1)S(1)}, u32[]{:S(2)}, u32[]{:S(2)}) collective-permute-start(bf16[96,512]{1,0:T(8,128)(2,1)S(1)} %reduce_sum.12), channel_id=1, source_target_pairs={{0,96},{32,0},{64,32},{96,64},{1,97},{33,1},{65,33},{97,65},{2,98}... | collective-permute-start | bytes 294920 | tf_op jit(solution)/shard_map/ppermute | solution.py:541
  110.6 2.3 %collective-permute-done.18 = bf16[96,512]{1,0:T(8,128)(2,1)S(1)} collective-permute-done((bf16[96,512]{1,0:T(8,128)(2,1)S(1)}, bf16[96,512]{1,0:T(8,128)(2,1)S(1)}, u32[]{:S(2)}, u32[]{:S(2)}) %collective-permute-start.18) | collective-permute-done | bytes 98336 | tf_op jit(solution)/shard_map/ppermute | solution.py:541
  112.9 0.7 collective-permute-done.19
  113.7 0.1 add_convert_fusion.2
  113.7 1.3 broadcast_in_dim.2
  115.0 5.0 %all-to-all-start.1 = ((bf16[16,96,512]{2,1,0:T(8,128)(2,1)}), bf16[16,96,512]{2,1,0:T(8,128)(2,1)S(1)}, u32[]{:S(2)}, u32[]{:S(2)}) async-start(bf16[16,96,512]{2,1,0:T(8,128)(2,1)} %broadcast_in_dim.2), calls=%async_computation.1 | async-start | bytes 3145728 | tf_op jit(solution)/shard_map/all_to_all | solution.py:544
  120.1 1.2 copy-done.21
  121.3 4.6 %shard_map.263 = bf16[227,2048]{1,0:T(8,128)(2,1)} custom-call(s32[2]{0:T(128)S(1)} %pad_add_fusion.refs_0_.refs_1_, s32[1,2048]{1,0:T(1,128)S(1)} %copy-done.18, bf16[227,2048]{1,0:T(8,128)(2,1)S(1)} %copy-done.21, bf16[227,128]{1,0:T(8,128)(2,1)S(1)} %collective-permute-done.14.refs_3_, bf16[227,128]{1,0:T(8,128)(2,1)S(1)} %collective-permute-done.15.refs_4_, ...), custom_call_target="tpu_custom_call" | custom-call | flops 5000000000 | bytes 5000000 | tf_op jit(solution)/shard_map/pallas_call | solution.py:108
  125.8 15.0 %all-to-all-done.1 = bf16[16,96,512]{2,1,0:T(8,128)(2,1)S(1)} async-done(((bf16[16,96,512]{2,1,0:T(8,128)(2,1)}), bf16[16,96,512]{2,1,0:T(8,128)(2,1)S(1)}, u32[]{:S(2)}, u32[]{:S(2)}) %all-to-all-start.1) | async-done | bytes 1572896 | tf_op jit(solution)/shard_map/all_to_all | solution.py:544
  140.8 3.9 %collective-permute-start.21 = (bf16[1536,512]{1,0:T(8,128)(2,1)S(1)}, bf16[1536,512]{1,0:T(8,128)(2,1)S(1)}, u32[]{:S(2)}, u32[]{:S(2)}) collective-permute-start(bf16[1536,512]{1,0:T(8,128)(2,1)S(1)} %bitcast.7), channel_id=1, source_target_pairs={{0,16},{16,0},{1,17},{17,1},{2,18},{18,2},{3,19},{19,3},{4,20},{20... | collective-permute-start | bytes 4718600 | tf_op jit(solution)/shard_map/ppermute | solution.py:448
  144.6 3.0 %collective-permute-done.21.refs_2_ = bf16[1536,512]{1,0:T(8,128)(2,1)S(1)} collective-permute-done((bf16[1536,512]{1,0:T(8,128)(2,1)S(1)}, bf16[1536,512]{1,0:T(8,128)(2,1)S(1)}, u32[]{:S(2)}, u32[]{:S(2)}) %collective-permute-start.21) | collective-permute-done | bytes 1572896 | tf_op jit(solution)/shard_map/ppermute | solution.py:448
  147.7 3.0 %shard_map.264 = (f32[227,512]{1,0:T(8,128)}, f32[512,512]{1,0:T(8,128)}, f32[512,512]{1,0:T(8,128)}, f32[512,512]{1,0:T(8,128)}, f32[256,512]{1,0:T(8,128)}, /*...) custom-call(s32[1]{0:T(128)} %bitcast.3.refs_0_, ...), custom_call_target="tpu_custom_call" | custom-call | flops 4000000000 | bytes 4000000 | tf_op jit(solution)/shard_map/pallas_call | solution.py:108
  (59 shorter events, 0.2 us)
Async XLA Ops:
  0.6 1.2 copy-start
  1.8 0.7 copy-start.17
  2.5 8.7 %copy-start.1 = (bf16[2048,227]{0,1:T(8,128)(2,1)S(1)}, bf16[2048,227]{0,1:T(8,128)(2,1)}, u32[]{:S(2)}) copy-start(bf16[2048,227]{0,1:T(8,128)(2,1)} %param.18) | copy-start | bytes 2789380
  2.5 8.7 %copy-start.2 = (bf16[512,512]{1,0:T(8,128)(2,1)S(1)}, bf16[512,512]{1,0:T(8,128)(2,1)}, u32[]{:S(2)}) copy-start(bf16[512,512]{1,0:T(8,128)(2,1)} %refs_20_.1) | copy-start | bytes 1572868
  2.5 8.7 %copy-start.3 = (bf16[512,512]{1,0:T(8,128)(2,1)S(1)}, bf16[512,512]{1,0:T(8,128)(2,1)}, u32[]{:S(2)}) copy-start(bf16[512,512]{1,0:T(8,128)(2,1)} %refs_17_.3) | copy-start | bytes 1572868
  2.5 8.7 %copy-start.11 = (bf16[256,512]{1,0:T(8,128)(2,1)S(1)}, bf16[256,512]{1,0:T(8,128)(2,1)}, u32[]{:S(2)}) copy-start(bf16[256,512]{1,0:T(8,128)(2,1)} %refs_18_.3) | copy-start | bytes 786436
  2.5 8.7 %copy-start.12 = (bf16[227,512]{1,0:T(8,128)(2,1)S(1)}, bf16[227,512]{1,0:T(8,128)(2,1)}, u32[]{:S(2)}) copy-start(bf16[227,512]{1,0:T(8,128)(2,1)} %refs_19_.1) | copy-start | bytes 697348
  2.6 8.7 %copy-start.13 = (s32[1,4096]{1,0:T(1,128)S(1)}, s32[1,4096]{1,0:T(1,128)}, u32[]{:S(2)}) copy-start(s32[1,4096]{1,0:T(1,128)} %refs_2_.7) | copy-start | bytes 49156
  2.6 8.7 %copy-start.14 = (s32[1,4096]{1,0:T(1,128)S(1)}, s32[1,4096]{1,0:T(1,128)}, u32[]{:S(2)}) copy-start(s32[1,4096]{1,0:T(1,128)} %refs_3_.1) | copy-start | bytes 49156
  2.6 8.7 %copy-start.18 = (s32[1,2048]{1,0:T(1,128)S(1)}, s32[1,2048]{1,0:T(1,128)}, u32[]{:S(2)}) copy-start(s32[1,2048]{1,0:T(1,128)} %refs_1_.7) | copy-start | bytes 24580
  3.3 15.3 %collective-permute-start = (bf16[227,128]{1,0:T(8,128)(2,1)S(1)}, bf16[227,128]{1,0:T(8,128)(2,1)S(1)}, u32[]{:S(2)}, u32[]{:S(2)}) collective-permute-start(bf16[227,128]{1,0:T(8,128)(2,1)S(1)} %get-tuple-element.70.refs_10_), channel_id=1, source_target_pairs={{0,16},{16,32},{32,48},{48,64},{64,80},{80,96},{96,112},{112,0},{1... | collective-permute-start | bytes 174344 | tf_op jit(solution)/shard_map/ppermute | solution.py:440
  6.3 12.3 %collective-permute-start.1 = (bf16[227,128]{1,0:T(8,128)(2,1)S(1)}, bf16[227,128]{1,0:T(8,128)(2,1)S(1)}, u32[]{:S(2)}, u32[]{:S(2)}) collective-permute-start(bf16[227,128]{1,0:T(8,128)(2,1)S(1)} %get-tuple-element.71.refs_9_), channel_id=1, source_target_pairs={{16,0},{32,16},{48,32},{64,48},{80,64},{96,80},{112,96},{0,112},{1... | collective-permute-start | bytes 174344 | tf_op jit(solution)/shard_map/ppermute | solution.py:441
  6.3 12.3 %collective-permute-start.2 = (bf16[227,128]{1,0:T(8,128)(2,1)S(1)}, bf16[227,128]{1,0:T(8,128)(2,1)S(1)}, u32[]{:S(2)}, u32[]{:S(2)}) collective-permute-start(bf16[227,128]{1,0:T(8,128)(2,1)S(1)} %get-tuple-element.72), channel_id=1, source_target_pairs={{0,1},{1,2},{2,3},{3,4},{4,5},{5,6},{6,7},{7,8},{8,9},{9,10},{10,1... | collective-permute-start | bytes 174344 | tf_op jit(solution)/shard_map/ppermute | solution.py:442
  7.5 11.1 %collective-permute-start.3 = (bf16[227,128]{1,0:T(8,128)(2,1)S(1)}, bf16[227,128]{1,0:T(8,128)(2,1)S(1)}, u32[]{:S(2)}, u32[]{:S(2)}) collective-permute-start(bf16[227,128]{1,0:T(8,128)(2,1)S(1)} %get-tuple-element.73), channel_id=1, source_target_pairs={{1,0},{2,1},{3,2},{4,3},{5,4},{6,5},{7,6},{8,7},{9,8},{10,9},{11,1... | collective-permute-start | bytes 174344 | tf_op jit(solution)/shard_map/ppermute | solution.py:443
  11.3 7.3 %copy-start.4 = (bf16[512,512]{1,0:T(8,128)(2,1)S(1)}, bf16[512,512]{1,0:T(8,128)(2,1)}, u32[]{:S(2)}) copy-start(bf16[512,512]{1,0:T(8,128)(2,1)} %refs_12_.5) | copy-start | bytes 1572868
  11.3 7.3 %copy-start.19 = (s32[1,2,2,32]{3,2,1,0:T(2,128)S(1)}, s32[1,2,2,32]{3,2,1,0:T(2,128)}, u32[]{:S(2)}) copy-start(s32[1,2,2,32]{3,2,1,0:T(2,128)} %refs_5_.3) | copy-start | bytes 1540
  18.7 18.7 %copy-start.5 = (bf16[256,512]{1,0:T(8,128)(2,1)S(1)}, bf16[256,512]{1,0:T(8,128)(2,1)}, u32[]{:S(2)}) copy-start(bf16[256,512]{1,0:T(8,128)(2,1)} %refs_9_.1) | copy-start | bytes 786436
  18.7 18.7 %copy-start.6 = (bf16[256,512]{1,0:T(8,128)(2,1)S(1)}, bf16[256,512]{1,0:T(8,128)(2,1)}, u32[]{:S(2)}) copy-start(bf16[256,512]{1,0:T(8,128)(2,1)} %refs_10_.1) | copy-start | bytes 786436
  18.7 18.7 %copy-start.7 = (bf16[512,256]{1,0:T(8,128)(2,1)S(1)}, bf16[512,256]{1,0:T(8,128)(2,1)}, u32[]{:S(2)}) copy-start(bf16[512,256]{1,0:T(8,128)(2,1)} %refs_11_.3) | copy-start | bytes 786436
  18.7 18.7 %copy-start.8 = (bf16[256,512]{1,0:T(8,128)(2,1)S(1)}, bf16[256,512]{1,0:T(8,128)(2,1)}, u32[]{:S(2)}) copy-start(bf16[256,512]{1,0:T(8,128)(2,1)} %refs_12_.4) | copy-start | bytes 786436
  18.7 18.7 %copy-start.9 = (bf16[512,256]{1,0:T(8,128)(2,1)S(1)}, bf16[512,256]{1,0:T(8,128)(2,1)}, u32[]{:S(2)}) copy-start(bf16[512,256]{1,0:T(8,128)(2,1)} %refs_13_.1) | copy-start | bytes 786436
  18.7 18.7 %copy-start.10 = (bf16[256,512]{1,0:T(8,128)(2,1)S(1)}, bf16[256,512]{1,0:T(8,128)(2,1)}, u32[]{:S(2)}) copy-start(bf16[256,512]{1,0:T(8,128)(2,1)} %refs_8_.1) | copy-start | bytes 786436
  18.7 18.7 %copy-start.15 = (s32[1,2048]{1,0:T(1,128)S(1)}, s32[1,2048]{1,0:T(1,128)}, u32[]{:S(2)}) copy-start(s32[1,2048]{1,0:T(1,128)} %refs_1_.6) | copy-start | bytes 24580
  18.8 18.7 %copy-start.16 = (s32[1,2048]{1,0:T(1,128)S(1)}, s32[1,2048]{1,0:T(1,128)}, u32[]{:S(2)}) copy-start(s32[1,2048]{1,0:T(1,128)} %refs_2_.6) | copy-start | bytes 24580
  29.0 7.2 %collective-permute-start.4 = (bf16[32,256]{1,0:T(8,128)(2,1)S(1)}, bf16[32,256]{1,0:T(8,128)(2,1)S(1)}, u32[]{:S(2)}, u32[]{:S(2)}) collective-permute-start(bf16[32,256]{1,0:T(8,128)(2,1)S(1)} %get-tuple-element.79), channel_id=1, source_target_pairs={{0,16},{16,32},{32,48},{48,64},{64,80},{80,96},{96,112},{112,0},{1... | collective-permute-start | bytes 49160 | tf_op jit(solution)/shard_map/ppermute | solution.py:440
  31.2 5.1 %collective-permute-start.5 = (bf16[32,256]{1,0:T(8,128)(2,1)S(1)}, bf16[32,256]{1,0:T(8,128)(2,1)S(1)}, u32[]{:S(2)}, u32[]{:S(2)}) collective-permute-start(bf16[32,256]{1,0:T(8,128)(2,1)S(1)} %get-tuple-element.80), channel_id=1, source_target_pairs={{16,0},{32,16},{48,32},{64,48},{80,64},{96,80},{112,96},{0,112},{1... | collective-permute-start | bytes 49160 | tf_op jit(solution)/shard_map/ppermute | solution.py:441
  31.4 5.9 %collective-permute-start.6 = (bf16[32,256]{1,0:T(8,128)(2,1)S(1)}, bf16[32,256]{1,0:T(8,128)(2,1)S(1)}, u32[]{:S(2)}, u32[]{:S(2)}) collective-permute-start(bf16[32,256]{1,0:T(8,128)(2,1)S(1)} %get-tuple-element.81), channel_id=1, source_target_pairs={{0,1},{1,2},{2,3},{3,4},{4,5},{5,6},{6,7},{7,8},{8,9},{9,10},{10,1... | collective-permute-start | bytes 49160 | tf_op jit(solution)/shard_map/ppermute | solution.py:442
  31.4 5.9 %collective-permute-start.7 = (bf16[32,256]{1,0:T(8,128)(2,1)S(1)}, bf16[32,256]{1,0:T(8,128)(2,1)S(1)}, u32[]{:S(2)}, u32[]{:S(2)}) collective-permute-start(bf16[32,256]{1,0:T(8,128)(2,1)S(1)} %get-tuple-element.82), channel_id=1, source_target_pairs={{1,0},{2,1},{3,2},{4,3},{5,4},{6,5},{7,6},{8,7},{9,8},{10,9},{11,1... | collective-permute-start | bytes 49160 | tf_op jit(solution)/shard_map/ppermute | solution.py:443
  44.2 10.6 %collective-permute-start.10 = (bf16[32,256]{1,0:T(8,128)(2,1)S(1)}, bf16[32,256]{1,0:T(8,128)(2,1)S(1)}, u32[]{:S(2)}, u32[]{:S(2)}) collective-permute-start(bf16[32,256]{1,0:T(8,128)(2,1)S(1)} %get-tuple-element.95), channel_id=1, source_target_pairs={{16,0},{32,16},{48,32},{64,48},{80,64},{96,80},{112,96},{0,112},{1... | collective-permute-start | bytes 49160 | tf_op jit(solution)/shard_map/ppermute | solution.py:441
  48.3 6.5 %collective-permute-start.11 = (bf16[32,256]{1,0:T(8,128)(2,1)S(1)}, bf16[32,256]{1,0:T(8,128)(2,1)S(1)}, u32[]{:S(2)}, u32[]{:S(2)}) collective-permute-start(bf16[32,256]{1,0:T(8,128)(2,1)S(1)} %get-tuple-element.96), channel_id=1, source_target_pairs={{0,1},{1,2},{2,3},{3,4},{4,5},{5,6},{6,7},{7,8},{8,9},{9,10},{10,1... | collective-permute-start | bytes 49160 | tf_op jit(solution)/shard_map/ppermute | solution.py:442
  48.3 6.5 %collective-permute-start.12 = (bf16[32,256]{1,0:T(8,128)(2,1)S(1)}, bf16[32,256]{1,0:T(8,128)(2,1)S(1)}, u32[]{:S(2)}, u32[]{:S(2)}) collective-permute-start(bf16[32,256]{1,0:T(8,128)(2,1)S(1)} %get-tuple-element.97), channel_id=1, source_target_pairs={{1,0},{2,1},{3,2},{4,3},{5,4},{6,5},{7,6},{8,7},{9,8},{10,9},{11,1... | collective-permute-start | bytes 49160 | tf_op jit(solution)/shard_map/ppermute | solution.py:443
  53.3 1.4 collective-permute-start.9
  54.1 18.6 %collective-permute-start.8 = (bf16[640,512]{1,0:T(8,128)(2,1)S(1)}, bf16[640,512]{1,0:T(8,128)(2,1)S(1)}, u32[]{:S(2)}, u32[]{:S(2)}) collective-permute-start(bf16[640,512]{1,0:T(8,128)(2,1)S(1)} %get-tuple-element.93), channel_id=1, source_target_pairs={{0,16},{16,0},{1,17},{17,1},{2,18},{18,2},{3,19},{19,3},{4,20},{20... | collective-permute-start | bytes 1966088 | tf_op jit(solution)/shard_map/ppermute | solution.py:448
  69.3 5.8 %copy-start.20 = (bf16[227,2048]{1,0:T(8,128)(2,1)}, bf16[227,2048]{1,0:T(8,128)(2,1)S(1)}, u32[]{:S(2)}) copy-start(bf16[227,2048]{1,0:T(8,128)(2,1)S(1)} %get-tuple-element.110.refs_2_) | copy-start | bytes 2789380
  69.3 5.5 %collective-permute-start.13 = (bf16[896,512]{1,0:T(8,128)(2,1)S(1)}, bf16[896,512]{1,0:T(8,128)(2,1)S(1)}, u32[]{:S(2)}, u32[]{:S(2)}) collective-permute-start(bf16[896,512]{1,0:T(8,128)(2,1)S(1)} %get-tuple-element.104), channel_id=1, source_target_pairs={{0,16},{16,0},{1,17},{17,1},{2,18},{18,2},{3,19},{19,3},{4,20},{20... | collective-permute-start | bytes 2752520 | tf_op jit(solution)/shard_map/ppermute | solution.py:448
  76.3 29.7 %all-to-all-start = ((bf16[16,96,512]{2,1,0:T(8,128)(2,1)}), bf16[16,96,512]{2,1,0:T(8,128)(2,1)}, u32[]{:S(2)}, u32[]{:S(2)}) async-start(bf16[16,96,512]{2,1,0:T(8,128)(2,1)} %bitcast.4), calls=%async_computation | async-start | bytes 3145728 | tf_op jit(solution)/shard_map/all_to_all | solution.py:534
  80.7 27.0 %collective-permute-start.14 = (bf16[227,128]{1,0:T(8,128)(2,1)S(1)}, bf16[227,128]{1,0:T(8,128)(2,1)S(1)}, u32[]{:S(2)}, u32[]{:S(2)}) collective-permute-start(bf16[227,128]{1,0:T(8,128)(2,1)S(1)} %get-tuple-element.105.refs_8_), channel_id=1, source_target_pairs={{0,16},{16,32},{32,48},{48,64},{64,80},{80,96},{96,112},{112,0},{1... | collective-permute-start | bytes 174344 | tf_op jit(solution)/shard_map/ppermute | solution.py:440
  80.8 27.0 %collective-permute-start.15 = (bf16[227,128]{1,0:T(8,128)(2,1)S(1)}, bf16[227,128]{1,0:T(8,128)(2,1)S(1)}, u32[]{:S(2)}, u32[]{:S(2)}) collective-permute-start(bf16[227,128]{1,0:T(8,128)(2,1)S(1)} %get-tuple-element.106.refs_7_), channel_id=1, source_target_pairs={{16,0},{32,16},{48,32},{64,48},{80,64},{96,80},{112,96},{0,112},{1... | collective-permute-start | bytes 174344 | tf_op jit(solution)/shard_map/ppermute | solution.py:441
  81.3 26.5 %collective-permute-start.16 = (bf16[227,128]{1,0:T(8,128)(2,1)S(1)}, bf16[227,128]{1,0:T(8,128)(2,1)S(1)}, u32[]{:S(2)}, u32[]{:S(2)}) collective-permute-start(bf16[227,128]{1,0:T(8,128)(2,1)S(1)} %get-tuple-element.107), channel_id=1, source_target_pairs={{0,1},{1,2},{2,3},{3,4},{4,5},{5,6},{6,7},{7,8},{8,9},{9,10},{10,1... | collective-permute-start | bytes 174344 | tf_op jit(solution)/shard_map/ppermute | solution.py:442
  82.6 25.1 %collective-permute-start.17 = (bf16[227,128]{1,0:T(8,128)(2,1)S(1)}, bf16[227,128]{1,0:T(8,128)(2,1)S(1)}, u32[]{:S(2)}, u32[]{:S(2)}) collective-permute-start(bf16[227,128]{1,0:T(8,128)(2,1)S(1)} %get-tuple-element.108), channel_id=1, source_target_pairs={{1,0},{2,1},{3,2},{4,3},{5,4},{6,5},{7,6},{8,7},{9,8},{10,9},{11,1... | collective-permute-start | bytes 174344 | tf_op jit(solution)/shard_map/ppermute | solution.py:443
  107.8 5.2 %collective-permute-start.18 = (bf16[96,512]{1,0:T(8,128)(2,1)S(1)}, bf16[96,512]{1,0:T(8,128)(2,1)S(1)}, u32[]{:S(2)}, u32[]{:S(2)}) collective-permute-start(bf16[96,512]{1,0:T(8,128)(2,1)S(1)} %reduce_sum.12), channel_id=1, source_target_pairs={{0,64},{32,96},{64,0},{96,32},{1,65},{33,97},{65,1},{97,33},{2,66}... | collective-permute-start | bytes 294920 | tf_op jit(solution)/shard_map/ppermute | solution.py:541
  107.8 5.8 %collective-permute-start.19 = (bf16[96,512]{1,0:T(8,128)(2,1)S(1)}, bf16[96,512]{1,0:T(8,128)(2,1)S(1)}, u32[]{:S(2)}, u32[]{:S(2)}) collective-permute-start(bf16[96,512]{1,0:T(8,128)(2,1)S(1)} %reduce_sum.12), channel_id=1, source_target_pairs={{0,32},{32,64},{64,96},{96,0},{1,33},{33,65},{65,97},{97,1},{2,34}... | collective-permute-start | bytes 294920 | tf_op jit(solution)/shard_map/ppermute | solution.py:541
  107.9 5.7 %collective-permute-start.20 = (bf16[96,512]{1,0:T(8,128)(2,1)S(1)}, bf16[96,512]{1,0:T(8,128)(2,1)S(1)}, u32[]{:S(2)}, u32[]{:S(2)}) collective-permute-start(bf16[96,512]{1,0:T(8,128)(2,1)S(1)} %reduce_sum.12), channel_id=1, source_target_pairs={{0,96},{32,0},{64,32},{96,64},{1,97},{33,1},{65,33},{97,65},{2,98}... | collective-permute-start | bytes 294920 | tf_op jit(solution)/shard_map/ppermute | solution.py:541
  115.0 25.7 %all-to-all-start.1 = ((bf16[16,96,512]{2,1,0:T(8,128)(2,1)}), bf16[16,96,512]{2,1,0:T(8,128)(2,1)S(1)}, u32[]{:S(2)}, u32[]{:S(2)}) async-start(bf16[16,96,512]{2,1,0:T(8,128)(2,1)} %broadcast_in_dim.2), calls=%async_computation.1 | async-start | bytes 3145728 | tf_op jit(solution)/shard_map/all_to_all | solution.py:544
  120.1 1.2 copy-start.21
  140.8 6.9 %collective-permute-start.21 = (bf16[1536,512]{1,0:T(8,128)(2,1)S(1)}, bf16[1536,512]{1,0:T(8,128)(2,1)S(1)}, u32[]{:S(2)}, u32[]{:S(2)}) collective-permute-start(bf16[1536,512]{1,0:T(8,128)(2,1)S(1)} %bitcast.7), channel_id=1, source_target_pairs={{0,16},{16,0},{1,17},{17,1},{2,18},{18,2},{3,19},{19,3},{4,20},{20... | collective-permute-start | bytes 4718600 | tf_op jit(solution)/shard_map/ppermute | solution.py:448

commit v2 on v1

--- a/solution.py
+++ b/solution.py
@@ -526,24 +526,24 @@
         ],
     )
     b_in = swap_cores(b_other)
-    back = trade(q0, q1, q2, q3)
     patches = lax.axis_size(PATCH)
     packed = (a_rows + b_rows) // 2
     pair = jnp.concatenate([a_mine.astype(F32) + a_in.astype(F32), b_mine.astype(F32) + b_in.astype(F32)], axis=0)
     pair = pair.astype(BF16).reshape(patches, packed // patches, dim)
     parts = lax.all_to_all(pair, PATCH, 0, 0)
     part = jnp.sum(parts.astype(F32), axis=0).astype(BF16)
-    part, *back = lax.optimization_barrier((part, *back))
+    away = [part] + [lax.ppermute(part, "z", [(i, (i + k) % 4) for i in range(4)]) for k in (1, 2, 3)]
+    away = [piece.astype(F32) for piece in away]
+    total = ((away[0] + away[2]) + (away[1] + away[3])).astype(BF16)
+    total, q0, q1, q2, q3 = lax.optimization_barrier((total, q0, q1, q2, q3))
+    back = trade(q0, q1, q2, q3)
+    mine = lax.all_to_all(jnp.broadcast_to(total[None], parts.shape), PATCH, 0, 0).reshape(packed, dim)
+    mine, *back = lax.optimization_barrier((mine, *back))
+    other = swap_cores(mine)
     ins = (flags, send_rows, rows_grad, *back, q0, q1)
     (grid_grad,) = call(
         place_kernel, [shape((chans, grid_rows), BF16)], 5, ins, scalars=1, scratch=[pltpu.VMEM((chans, grid_rows), BF16)]
     )
-    away = [part] + [lax.ppermute(part, "z", [(i, (i + k) % 4) for i in range(4)]) for k in (1, 2, 3)]
-    away = [piece.astype(F32) for piece in away]
-    total = ((away[0] + away[2]) + (away[1] + away[3])).astype(BF16)
-    mine = lax.all_to_all(jnp.broadcast_to(total[None], parts.shape), PATCH, 0, 0).reshape(packed, dim)
-    mine, grid_grad = lax.optimization_barrier((mine, grid_grad))
-    other = swap_cores(mine)
     outs = [shape((chans, dim), F32)] + [shape((dim, dim), F32)] * 3 + [shape((half, dim), F32)] * 2
     outs += [shape((dim, half), F32), shape((half, dim), F32), shape((dim, half), F32)]
     totals = call(functools.partial(unpack_kernel, a_rows), outs, 4, (core, mine, other), scalars=1, sent=tuple(range(9)))

time: 151 us -> 148 us (0.980)
  blocking collectives: 0 us -> 25.5 us
  waiting for transfers between devices: 44.1 us -> 22.5 us
  starting transfers between devices: 49.8 us -> 45.1 us
  other arithmetic: 3.47 us -> 0.89 us
    all_to_all x0 -> x1, blocking collectives: none -> 25.5 us  [body(): parts = lax.all_to_all(pair, PATCH, 0, 0)]
    all_to_all x1 -> x0, waiting for transfers between devices: 20 us -> none  [body(): parts = lax.all_to_all(pair, PATCH, 0, 0)]
    ppermute x4, waiting for transfers between devices: 1.12 us -> 16.5 us  [trade(): lax.ppermute(east, PATCH, right)]
    all_to_all x1, waiting for transfers between devices: 15 us -> 0.01 us  [body(): lax.all_to_all(jnp.broadcast_to(total[None], parts.shape), PATCH, 0, 0)]
    ppermute x4, starting transfers between devices: 5.23 us -> 10.5 us  [trade(): lax.ppermute(above, BAND, up)]
    all_to_all x1 -> x0, starting transfers between devices: 4.4 us -> none  [body(): parts = lax.all_to_all(pair, PATCH, 0, 0)]
    ppermute x3, waiting for transfers between devices: 4.95 us -> 1.93 us  [swap_cores(): return lax.ppermute(value, 'core', [(0, 1), (1, 0)])]
    ppermute x4, starting transfers between devices: 4.86 us -> 2.04 us  [trade(): lax.ppermute(below, BAND, down)]
  transfers between devices with their start and end apart: 24 -> 23, of which waited for: 7 -> 6; matrix products, arithmetic and copies ran while one was open for 1% -> 0% of each run, Pallas kernels for 18% -> 18%
where the time goes in v2:
time: 148 us; the launch traced here: 147 us
  Pallas kernels  47.6 us (32%)
  starting transfers between devices  45.1 us (30%)
  blocking collectives  25.5 us (17%)
  waiting for transfers between devices  22.5 us (15%)
  local copies, waits for them, and re-layouts  4.51 us (3%)
    pallas_call x8, Pallas kernels, call(): pl.pallas_call(run, out_shape=outs, in_specs=[pl.BlockSpec(memory_space=s...  47.6 us
    all_to_all x1, blocking collectives, body(): parts = lax.all_to_all(pair, PATCH, 0, 0)  25.5 us
    ppermute x4, starting transfers between devices, trade(): lax.ppermute(west, PATCH, left)  16.8 us
    ppermute x4, waiting for transfers between devices, trade(): lax.ppermute(east, PATCH, right)  16.5 us
    ppermute x4, starting transfers between devices, trade(): lax.ppermute(above, BAND, up)  10.5 us
    ppermute x3, starting transfers between devices, swap_cores(): return lax.ppermute(value, 'core', [(0, 1), (1, 0)])  5.88 us
    ppermute x3, waiting for transfers between devices, body(): lax.ppermute(part, 'z', [(i, (i + k) % 4) for i in range(4)])  4.06 us
    all_to_all x1, starting transfers between devices, body(): lax.all_to_all(jnp.broadcast_to(total[None], parts.shape), PATCH, 0, 0)  3.71 us
  transfers between devices with their start and end apart: 23, of which 6 were waited for; matrix products, arithmetic and copies ran while one was open for 0% of the time, Pallas kernels for 18%

profile of v2, /device:TPU:1, one launch (start us, length us, event | category | flops | bytes accessed | tf_op | source)
XLA Modules:
  0.0 147.3 jit_solution(14354222746056211500)
XLA Ops:
  0.7 1.2 copy-done
  1.8 0.7 copy-done.17
  2.6 0.7 shard_map.258
  3.3 3.0 %collective-permute-start = (bf16[227,128]{1,0:T(8,128)(2,1)S(1)}, bf16[227,128]{1,0:T(8,128)(2,1)S(1)}, u32[]{:S(2)}, u32[]{:S(2)}) collective-permute-start(bf16[227,128]{1,0:T(8,128)(2,1)S(1)} %get-tuple-element.73.refs_10_), channel_id=1, source_target_pairs={{0,16},{16,32},{32,48},{48,64},{64,80},{80,96},{96,112},{112,0},{1... | collective-permute-start | bytes 174344 | tf_op jit(solution)/shard_map/ppermute | solution.py:440
  6.3 1.2 collective-permute-start.2
  7.5 3.7 %collective-permute-start.3 = (bf16[227,128]{1,0:T(8,128)(2,1)S(1)}, bf16[227,128]{1,0:T(8,128)(2,1)S(1)}, u32[]{:S(2)}, u32[]{:S(2)}) collective-permute-start(bf16[227,128]{1,0:T(8,128)(2,1)S(1)} %get-tuple-element.76), channel_id=1, source_target_pairs={{1,0},{2,1},{3,2},{4,3},{5,4},{6,5},{7,6},{8,7},{9,8},{10,9},{11,1... | collective-permute-start | bytes 174344 | tf_op jit(solution)/shard_map/ppermute | solution.py:443
  11.3 7.2 %shard_map.257 = (bf16[227,1536]{1,0:T(8,128)(2,1)S(1)}, bf16[1536,512]{1,0:T(8,128)(2,1)S(1)}, bf16[256,512]{1,0:T(8,128)(2,1)S(1)}, bf16[2048,128]{1,0:T(8,128)(2,1)S(1)}, s32[1,2048]{1,0:T(1,128)S(1)}) custom-call(s32[1,2048]{1,0:T(1,128)S(1)} %copy-done.18, s32[1,4096]{1,0:T(1,128)S(1)} %copy-done.13, s32[1,4096]{1,0:T(1,128)S(1)} %copy-done.14, ...), custom_call_target="tpu_custom_call" | custom-call | flops 6000000000 | bytes 6000000 | tf_op jit(solution)/shard_map/pallas_call | solution.py:108
  18.5 0.1 pad_add_fusion.refs_0_.refs_1_
  18.7 0.0 copy-start.6
  18.7 0.0 copy-start.7
  18.8 10.2 %shard_map.259 = (bf16[227,2048]{1,0:T(8,128)(2,1)S(1)}, bf16[2048,512]{1,0:T(8,128)(2,1)S(1)}, bf16[2048,512]{1,0:T(8,128)(2,1)S(1)}, bf16[256,512]{1,0:T(8,128...) custom-call(s32[2]{0:T(128)S(1)} %pad_add_fusion.refs_0_.refs_1_, ...), custom_call_target="tpu_custom_call" | custom-call | flops 12000000000 | bytes 12000000 | tf_op jit(solution)/shard_map/pallas_call | solution.py:108
  29.0 2.2 %collective-permute-start.4 = (bf16[32,256]{1,0:T(8,128)(2,1)S(1)}, bf16[32,256]{1,0:T(8,128)(2,1)S(1)}, u32[]{:S(2)}, u32[]{:S(2)}) collective-permute-start(bf16[32,256]{1,0:T(8,128)(2,1)S(1)} %get-tuple-element.82), channel_id=1, source_target_pairs={{0,16},{16,32},{32,48},{48,64},{64,80},{80,96},{96,112},{112,0},{1... | collective-permute-start | bytes 49160 | tf_op jit(solution)/shard_map/ppermute | solution.py:440
  31.2 0.3 collective-permute-start.5
  31.4 4.8 %collective-permute-start.7 = (bf16[32,256]{1,0:T(8,128)(2,1)S(1)}, bf16[32,256]{1,0:T(8,128)(2,1)S(1)}, u32[]{:S(2)}, u32[]{:S(2)}) collective-permute-start(bf16[32,256]{1,0:T(8,128)(2,1)S(1)} %get-tuple-element.85), channel_id=1, source_target_pairs={{1,0},{2,1},{3,2},{4,3},{5,4},{6,5},{7,6},{8,7},{9,8},{10,9},{11,1... | collective-permute-start | bytes 49160 | tf_op jit(solution)/shard_map/ppermute | solution.py:443
  36.2 1.1 collective-permute-done.6.refs_7_
  37.4 6.7 %shard_map.260 = (bf16[32,256]{1,0:T(8,128)(2,1)S(1)}, bf16[32,256]{1,0:T(8,128)(2,1)S(1)}, bf16[32,256]{1,0:T(8,128)(2,1)S(1)}, bf16[32,256]{1,0:T(8,128)(2,1)S...) custom-call(s32[2]{0:T(128)S(1)} %pad_add_fusion.refs_0_.refs_1_, ...), custom_call_target="tpu_custom_call" | custom-call | flops 6000000000 | bytes 6000000 | tf_op jit(solution)/shard_map/pallas_call | solution.py:108
  44.1 0.1 collective-permute-start.10
  44.2 4.9 %collective-permute-start.11 = (bf16[32,256]{1,0:T(8,128)(2,1)S(1)}, bf16[32,256]{1,0:T(8,128)(2,1)S(1)}, u32[]{:S(2)}, u32[]{:S(2)}) collective-permute-start(bf16[32,256]{1,0:T(8,128)(2,1)S(1)} %get-tuple-element.89), channel_id=1, source_target_pairs={{1,0},{2,1},{3,2},{4,3},{5,4},{6,5},{7,6},{8,7},{9,8},{10,9},{11,1... | collective-permute-start | bytes 49160 | tf_op jit(solution)/shard_map/ppermute | solution.py:443
  49.1 3.2 %collective-permute-start.8 = (bf16[32,256]{1,0:T(8,128)(2,1)S(1)}, bf16[32,256]{1,0:T(8,128)(2,1)S(1)}, u32[]{:S(2)}, u32[]{:S(2)}) collective-permute-start(bf16[32,256]{1,0:T(8,128)(2,1)S(1)} %get-tuple-element.86), channel_id=1, source_target_pairs={{0,16},{16,32},{32,48},{48,64},{64,80},{80,96},{96,112},{112,0},{1... | collective-permute-start | bytes 49160 | tf_op jit(solution)/shard_map/ppermute | solution.py:440
  52.3 1.4 collective-permute-start.9
  53.7 0.8 shard_map.261
  54.5 3.0 %collective-permute-start.12 = (bf16[640,512]{1,0:T(8,128)(2,1)S(1)}, bf16[640,512]{1,0:T(8,128)(2,1)S(1)}, u32[]{:S(2)}, u32[]{:S(2)}) collective-permute-start(bf16[640,512]{1,0:T(8,128)(2,1)S(1)} %get-tuple-element.106), channel_id=1, source_target_pairs={{0,16},{16,0},{1,17},{17,1},{2,18},{18,2},{3,19},{19,3},{4,20},{20... | collective-permute-start | bytes 1966088 | tf_op jit(solution)/shard_map/ppermute | solution.py:448
  57.6 14.4 %shard_map.262 = (bf16[227,2048]{1,0:T(8,128)(2,1)S(1)}, bf16[227,128]{1,0:T(8,128)(2,1)S(1)}, bf16[227,128]{1,0:T(8,128)(2,1)S(1)}, bf16[227,128]{1,0:T(8,128)(...) custom-call(s32[1]{0:T(128)} %bitcast.2.refs_0_, ...), custom_call_target="tpu_custom_call" | custom-call | flops 14000000000 | bytes 14000000 | tf_op jit(solution)/shard_map/pallas_call | solution.py:108
  72.0 0.6 collective-permute-start.13
  72.6 0.2 add_convert_fusion.1
  72.8 1.9 %collective-permute-done.13 = bf16[896,512]{1,0:T(8,128)(2,1)S(1)} collective-permute-done((bf16[896,512]{1,0:T(8,128)(2,1)S(1)}, bf16[896,512]{1,0:T(8,128)(2,1)S(1)}, u32[]{:S(2)}, u32[]{:S(2)}) %collective-permute-start.13) | collective-permute-done | bytes 917536 | tf_op jit(solution)/shard_map/ppermute | solution.py:448
  74.7 0.3 add_convert_fusion
  75.0 0.1 pad_maximum_fusion
  75.1 25.5 %all_to_all.10 = bf16[16,96,512]{2,1,0:T(8,128)(2,1)S(1)} all-to-all(bf16[16,96,512]{2,1,0:T(8,128)(2,1)S(1)} %bitcast.11), channel_id=1, replica_groups=mesh['z'=4,'core'=2,'y'=4,'x'=4] {'y','x'}, dimensions={0} | all-to-all | bytes 3145728 | tf_op jit(solution)/shard_map/all_to_all | solution.py:533
  100.6 0.2 reduce_sum.12
  100.8 0.7 collective-permute-start.14
  101.5 2.4 %collective-permute-start.15 = (bf16[96,512]{1,0:T(8,128)(2,1)S(1)}, bf16[96,512]{1,0:T(8,128)(2,1)S(1)}, u32[]{:S(2)}, u32[]{:S(2)}) collective-permute-start(bf16[96,512]{1,0:T(8,128)(2,1)S(1)} %reduce_sum.12), channel_id=1, source_target_pairs={{0,32},{32,64},{64,96},{96,0},{1,33},{33,65},{65,97},{97,1},{2,34}... | collective-permute-start | bytes 294920 | tf_op jit(solution)/shard_map/ppermute | solution.py:535
  103.9 0.3 collective-permute-start.16
  104.2 1.7 %collective-permute-done.14 = bf16[96,512]{1,0:T(8,128)(2,1)S(1)} collective-permute-done((bf16[96,512]{1,0:T(8,128)(2,1)S(1)}, bf16[96,512]{1,0:T(8,128)(2,1)S(1)}, u32[]{:S(2)}, u32[]{:S(2)}) %collective-permute-start.14) | collective-permute-done | bytes 98336 | tf_op jit(solution)/shard_map/ppermute | solution.py:535
  105.9 1.0 collective-permute-done.15
  106.9 1.3 collective-permute-done.16
  108.3 0.1 add_convert_fusion.2
  108.3 1.3 broadcast_in_dim.2
  109.7 3.7 %all-to-all-start.1 = ((bf16[16,96,512]{2,1,0:T(8,128)(2,1)}), bf16[16,96,512]{2,1,0:T(8,128)(2,1)S(1)}, u32[]{:S(2)}, u32[]{:S(2)}) async-start(bf16[16,96,512]{2,1,0:T(8,128)(2,1)} %broadcast_in_dim.2), calls=%async_computation.1 | async-start | bytes 3145728 | tf_op jit(solution)/shard_map/all_to_all | solution.py:540
  113.4 2.1 %collective-permute-start.17 = (bf16[227,128]{1,0:T(8,128)(2,1)S(1)}, bf16[227,128]{1,0:T(8,128)(2,1)S(1)}, u32[]{:S(2)}, u32[]{:S(2)}) collective-permute-start(bf16[227,128]{1,0:T(8,128)(2,1)S(1)} %get-tuple-element.114.refs_8_), channel_id=1, source_target_pairs={{0,16},{16,32},{32,48},{48,64},{64,80},{80,96},{96,112},{112,0},{1... | collective-permute-start | bytes 174344 | tf_op jit(solution)/shard_map/ppermute | solution.py:440
  115.5 0.3 collective-permute-start.18
  115.8 1.5 %collective-permute-start.19 = (bf16[227,128]{1,0:T(8,128)(2,1)S(1)}, bf16[227,128]{1,0:T(8,128)(2,1)S(1)}, u32[]{:S(2)}, u32[]{:S(2)}) collective-permute-start(bf16[227,128]{1,0:T(8,128)(2,1)S(1)} %get-tuple-element.116), channel_id=1, source_target_pairs={{0,1},{1,2},{2,3},{3,4},{4,5},{5,6},{6,7},{7,8},{8,9},{9,10},{10,1... | collective-permute-start | bytes 174344 | tf_op jit(solution)/shard_map/ppermute | solution.py:442
  117.3 3.4 %collective-permute-start.20 = (bf16[227,128]{1,0:T(8,128)(2,1)S(1)}, bf16[227,128]{1,0:T(8,128)(2,1)S(1)}, u32[]{:S(2)}, u32[]{:S(2)}) collective-permute-start(bf16[227,128]{1,0:T(8,128)(2,1)S(1)} %get-tuple-element.117), channel_id=1, source_target_pairs={{1,0},{2,1},{3,2},{4,3},{5,4},{6,5},{7,6},{8,7},{9,8},{10,9},{11,1... | collective-permute-start | bytes 174344 | tf_op jit(solution)/shard_map/ppermute | solution.py:443
  120.8 15.3 %collective-permute-done.19.refs_5_ = bf16[227,128]{1,0:T(8,128)(2,1)S(1)} collective-permute-done((bf16[227,128]{1,0:T(8,128)(2,1)S(1)}, bf16[227,128]{1,0:T(8,128)(2,1)S(1)}, u32[]{:S(2)}, u32[]{:S(2)}) %collective-permute-start.19) | collective-permute-done | bytes 58144 | tf_op jit(solution)/shard_map/ppermute | solution.py:442
  136.1 2.3 %collective-permute-start.21 = (bf16[1536,512]{1,0:T(8,128)(2,1)S(1)}, bf16[1536,512]{1,0:T(8,128)(2,1)S(1)}, u32[]{:S(2)}, u32[]{:S(2)}) collective-permute-start(bf16[1536,512]{1,0:T(8,128)(2,1)S(1)} %bitcast.7), channel_id=1, source_target_pairs={{0,16},{16,0},{1,17},{17,1},{2,18},{18,2},{3,19},{19,3},{4,20},{20... | collective-permute-start | bytes 4718600 | tf_op jit(solution)/shard_map/ppermute | solution.py:448
  138.4 1.2 copy-done.21
  139.6 4.6 %shard_map.263 = bf16[227,2048]{1,0:T(8,128)(2,1)} custom-call(s32[2]{0:T(128)S(1)} %pad_add_fusion.refs_0_.refs_1_, s32[1,2048]{1,0:T(1,128)S(1)} %copy-done.18, bf16[227,2048]{1,0:T(8,128)(2,1)S(1)} %copy-done.21, bf16[227,128]{1,0:T(8,128)(2,1)S(1)} %collective-permute-done.17.refs_3_, bf16[227,128]{1,0:T(8,128)(2,1)S(1)} %collective-permute-done.18.refs_4_, ...), custom_call_target="tpu_custom_call" | custom-call | flops 5000000000 | bytes 5000000 | tf_op jit(solution)/shard_map/pallas_call | solution.py:108
  144.1 3.0 %shard_map.264 = (f32[227,512]{1,0:T(8,128)}, f32[512,512]{1,0:T(8,128)}, f32[512,512]{1,0:T(8,128)}, f32[512,512]{1,0:T(8,128)}, f32[256,512]{1,0:T(8,128)}, /*...) custom-call(s32[1]{0:T(128)} %bitcast.2.refs_0_, ...), custom_call_target="tpu_custom_call" | custom-call | flops 4000000000 | bytes 4000000 | tf_op jit(solution)/shard_map/pallas_call | solution.py:108
  (58 shorter events, 0.1 us)
Async XLA Ops:
  0.6 1.2 copy-start
  1.8 0.7 copy-start.17
  2.5 8.7 %copy-start.1 = (bf16[2048,227]{0,1:T(8,128)(2,1)S(1)}, bf16[2048,227]{0,1:T(8,128)(2,1)}, u32[]{:S(2)}) copy-start(bf16[2048,227]{0,1:T(8,128)(2,1)} %param.18) | copy-start | bytes 2789380
  2.5 8.7 %copy-start.2 = (bf16[512,512]{1,0:T(8,128)(2,1)S(1)}, bf16[512,512]{1,0:T(8,128)(2,1)}, u32[]{:S(2)}) copy-start(bf16[512,512]{1,0:T(8,128)(2,1)} %refs_20_.1) | copy-start | bytes 1572868
  2.5 8.7 %copy-start.3 = (bf16[512,512]{1,0:T(8,128)(2,1)S(1)}, bf16[512,512]{1,0:T(8,128)(2,1)}, u32[]{:S(2)}) copy-start(bf16[512,512]{1,0:T(8,128)(2,1)} %refs_17_.3) | copy-start | bytes 1572868
  2.5 8.7 %copy-start.11 = (bf16[256,512]{1,0:T(8,128)(2,1)S(1)}, bf16[256,512]{1,0:T(8,128)(2,1)}, u32[]{:S(2)}) copy-start(bf16[256,512]{1,0:T(8,128)(2,1)} %refs_18_.3) | copy-start | bytes 786436
  2.5 8.7 %copy-start.12 = (bf16[227,512]{1,0:T(8,128)(2,1)S(1)}, bf16[227,512]{1,0:T(8,128)(2,1)}, u32[]{:S(2)}) copy-start(bf16[227,512]{1,0:T(8,128)(2,1)} %refs_19_.1) | copy-start | bytes 697348
  2.6 8.7 %copy-start.13 = (s32[1,4096]{1,0:T(1,128)S(1)}, s32[1,4096]{1,0:T(1,128)}, u32[]{:S(2)}) copy-start(s32[1,4096]{1,0:T(1,128)} %refs_2_.7) | copy-start | bytes 49156
  2.6 8.7 %copy-start.14 = (s32[1,4096]{1,0:T(1,128)S(1)}, s32[1,4096]{1,0:T(1,128)}, u32[]{:S(2)}) copy-start(s32[1,4096]{1,0:T(1,128)} %refs_3_.1) | copy-start | bytes 49156
  2.6 8.7 %copy-start.18 = (s32[1,2048]{1,0:T(1,128)S(1)}, s32[1,2048]{1,0:T(1,128)}, u32[]{:S(2)}) copy-start(s32[1,2048]{1,0:T(1,128)} %refs_1_.7) | copy-start | bytes 24580
  3.3 15.3 %collective-permute-start = (bf16[227,128]{1,0:T(8,128)(2,1)S(1)}, bf16[227,128]{1,0:T(8,128)(2,1)S(1)}, u32[]{:S(2)}, u32[]{:S(2)}) collective-permute-start(bf16[227,128]{1,0:T(8,128)(2,1)S(1)} %get-tuple-element.73.refs_10_), channel_id=1, source_target_pairs={{0,16},{16,32},{32,48},{48,64},{64,80},{80,96},{96,112},{112,0},{1... | collective-permute-start | bytes 174344 | tf_op jit(solution)/shard_map/ppermute | solution.py:440
  6.3 12.3 %collective-permute-start.1 = (bf16[227,128]{1,0:T(8,128)(2,1)S(1)}, bf16[227,128]{1,0:T(8,128)(2,1)S(1)}, u32[]{:S(2)}, u32[]{:S(2)}) collective-permute-start(bf16[227,128]{1,0:T(8,128)(2,1)S(1)} %get-tuple-element.74.refs_9_), channel_id=1, source_target_pairs={{16,0},{32,16},{48,32},{64,48},{80,64},{96,80},{112,96},{0,112},{1... | collective-permute-start | bytes 174344 | tf_op jit(solution)/shard_map/ppermute | solution.py:441
  6.3 12.3 %collective-permute-start.2 = (bf16[227,128]{1,0:T(8,128)(2,1)S(1)}, bf16[227,128]{1,0:T(8,128)(2,1)S(1)}, u32[]{:S(2)}, u32[]{:S(2)}) collective-permute-start(bf16[227,128]{1,0:T(8,128)(2,1)S(1)} %get-tuple-element.75), channel_id=1, source_target_pairs={{0,1},{1,2},{2,3},{3,4},{4,5},{5,6},{6,7},{7,8},{8,9},{9,10},{10,1... | collective-permute-start | bytes 174344 | tf_op jit(solution)/shard_map/ppermute | solution.py:442
  7.5 11.1 %collective-permute-start.3 = (bf16[227,128]{1,0:T(8,128)(2,1)S(1)}, bf16[227,128]{1,0:T(8,128)(2,1)S(1)}, u32[]{:S(2)}, u32[]{:S(2)}) collective-permute-start(bf16[227,128]{1,0:T(8,128)(2,1)S(1)} %get-tuple-element.76), channel_id=1, source_target_pairs={{1,0},{2,1},{3,2},{4,3},{5,4},{6,5},{7,6},{8,7},{9,8},{10,9},{11,1... | collective-permute-start | bytes 174344 | tf_op jit(solution)/shard_map/ppermute | solution.py:443
  11.3 7.3 %copy-start.4 = (bf16[512,512]{1,0:T(8,128)(2,1)S(1)}, bf16[512,512]{1,0:T(8,128)(2,1)}, u32[]{:S(2)}) copy-start(bf16[512,512]{1,0:T(8,128)(2,1)} %refs_12_.5) | copy-start | bytes 1572868
  11.3 7.3 %copy-start.19 = (s32[1,2,2,32]{3,2,1,0:T(2,128)S(1)}, s32[1,2,2,32]{3,2,1,0:T(2,128)}, u32[]{:S(2)}) copy-start(s32[1,2,2,32]{3,2,1,0:T(2,128)} %refs_5_.3) | copy-start | bytes 1540
  18.7 18.7 %copy-start.5 = (bf16[256,512]{1,0:T(8,128)(2,1)S(1)}, bf16[256,512]{1,0:T(8,128)(2,1)}, u32[]{:S(2)}) copy-start(bf16[256,512]{1,0:T(8,128)(2,1)} %refs_9_.1) | copy-start | bytes 786436
  18.7 18.7 %copy-start.6 = (bf16[256,512]{1,0:T(8,128)(2,1)S(1)}, bf16[256,512]{1,0:T(8,128)(2,1)}, u32[]{:S(2)}) copy-start(bf16[256,512]{1,0:T(8,128)(2,1)} %refs_10_.1) | copy-start | bytes 786436
  18.7 18.7 %copy-start.7 = (bf16[512,256]{1,0:T(8,128)(2,1)S(1)}, bf16[512,256]{1,0:T(8,128)(2,1)}, u32[]{:S(2)}) copy-start(bf16[512,256]{1,0:T(8,128)(2,1)} %refs_11_.3) | copy-start | bytes 786436
  18.7 18.7 %copy-start.8 = (bf16[256,512]{1,0:T(8,128)(2,1)S(1)}, bf16[256,512]{1,0:T(8,128)(2,1)}, u32[]{:S(2)}) copy-start(bf16[256,512]{1,0:T(8,128)(2,1)} %refs_12_.4) | copy-start | bytes 786436
  18.7 18.7 %copy-start.9 = (bf16[512,256]{1,0:T(8,128)(2,1)S(1)}, bf16[512,256]{1,0:T(8,128)(2,1)}, u32[]{:S(2)}) copy-start(bf16[512,256]{1,0:T(8,128)(2,1)} %refs_13_.1) | copy-start | bytes 786436
  18.7 18.7 %copy-start.10 = (bf16[256,512]{1,0:T(8,128)(2,1)S(1)}, bf16[256,512]{1,0:T(8,128)(2,1)}, u32[]{:S(2)}) copy-start(bf16[256,512]{1,0:T(8,128)(2,1)} %refs_8_.1) | copy-start | bytes 786436
  18.7 18.7 %copy-start.15 = (s32[1,2048]{1,0:T(1,128)S(1)}, s32[1,2048]{1,0:T(1,128)}, u32[]{:S(2)}) copy-start(s32[1,2048]{1,0:T(1,128)} %refs_1_.6) | copy-start | bytes 24580
  18.8 18.7 %copy-start.16 = (s32[1,2048]{1,0:T(1,128)S(1)}, s32[1,2048]{1,0:T(1,128)}, u32[]{:S(2)}) copy-start(s32[1,2048]{1,0:T(1,128)} %refs_2_.6) | copy-start | bytes 24580
  29.0 7.2 %collective-permute-start.4 = (bf16[32,256]{1,0:T(8,128)(2,1)S(1)}, bf16[32,256]{1,0:T(8,128)(2,1)S(1)}, u32[]{:S(2)}, u32[]{:S(2)}) collective-permute-start(bf16[32,256]{1,0:T(8,128)(2,1)S(1)} %get-tuple-element.82), channel_id=1, source_target_pairs={{0,16},{16,32},{32,48},{48,64},{64,80},{80,96},{96,112},{112,0},{1... | collective-permute-start | bytes 49160 | tf_op jit(solution)/shard_map/ppermute | solution.py:440
  31.2 5.1 %collective-permute-start.5 = (bf16[32,256]{1,0:T(8,128)(2,1)S(1)}, bf16[32,256]{1,0:T(8,128)(2,1)S(1)}, u32[]{:S(2)}, u32[]{:S(2)}) collective-permute-start(bf16[32,256]{1,0:T(8,128)(2,1)S(1)} %get-tuple-element.83), channel_id=1, source_target_pairs={{16,0},{32,16},{48,32},{64,48},{80,64},{96,80},{112,96},{0,112},{1... | collective-permute-start | bytes 49160 | tf_op jit(solution)/shard_map/ppermute | solution.py:441
  31.4 5.9 %collective-permute-start.6 = (bf16[32,256]{1,0:T(8,128)(2,1)S(1)}, bf16[32,256]{1,0:T(8,128)(2,1)S(1)}, u32[]{:S(2)}, u32[]{:S(2)}) collective-permute-start(bf16[32,256]{1,0:T(8,128)(2,1)S(1)} %get-tuple-element.84), channel_id=1, source_target_pairs={{0,1},{1,2},{2,3},{3,4},{4,5},{5,6},{6,7},{7,8},{8,9},{9,10},{10,1... | collective-permute-start | bytes 49160 | tf_op jit(solution)/shard_map/ppermute | solution.py:442
  31.4 5.9 %collective-permute-start.7 = (bf16[32,256]{1,0:T(8,128)(2,1)S(1)}, bf16[32,256]{1,0:T(8,128)(2,1)S(1)}, u32[]{:S(2)}, u32[]{:S(2)}) collective-permute-start(bf16[32,256]{1,0:T(8,128)(2,1)S(1)} %get-tuple-element.85), channel_id=1, source_target_pairs={{1,0},{2,1},{3,2},{4,3},{5,4},{6,5},{7,6},{8,7},{9,8},{10,9},{11,1... | collective-permute-start | bytes 49160 | tf_op jit(solution)/shard_map/ppermute | solution.py:443
  44.1 13.4 %collective-permute-start.10 = (bf16[32,256]{1,0:T(8,128)(2,1)S(1)}, bf16[32,256]{1,0:T(8,128)(2,1)S(1)}, u32[]{:S(2)}, u32[]{:S(2)}) collective-permute-start(bf16[32,256]{1,0:T(8,128)(2,1)S(1)} %get-tuple-element.88), channel_id=1, source_target_pairs={{0,1},{1,2},{2,3},{3,4},{4,5},{5,6},{6,7},{7,8},{8,9},{9,10},{10,1... | collective-permute-start | bytes 49160 | tf_op jit(solution)/shard_map/ppermute | solution.py:442
  44.2 13.3 %collective-permute-start.11 = (bf16[32,256]{1,0:T(8,128)(2,1)S(1)}, bf16[32,256]{1,0:T(8,128)(2,1)S(1)}, u32[]{:S(2)}, u32[]{:S(2)}) collective-permute-start(bf16[32,256]{1,0:T(8,128)(2,1)S(1)} %get-tuple-element.89), channel_id=1, source_target_pairs={{1,0},{2,1},{3,2},{4,3},{5,4},{6,5},{7,6},{8,7},{9,8},{10,9},{11,1... | collective-permute-start | bytes 49160 | tf_op jit(solution)/shard_map/ppermute | solution.py:443
  49.1 8.5 %collective-permute-start.8 = (bf16[32,256]{1,0:T(8,128)(2,1)S(1)}, bf16[32,256]{1,0:T(8,128)(2,1)S(1)}, u32[]{:S(2)}, u32[]{:S(2)}) collective-permute-start(bf16[32,256]{1,0:T(8,128)(2,1)S(1)} %get-tuple-element.86), channel_id=1, source_target_pairs={{0,16},{16,32},{32,48},{48,64},{64,80},{80,96},{96,112},{112,0},{1... | collective-permute-start | bytes 49160 | tf_op jit(solution)/shard_map/ppermute | solution.py:440
  52.3 5.3 %collective-permute-start.9 = (bf16[32,256]{1,0:T(8,128)(2,1)S(1)}, bf16[32,256]{1,0:T(8,128)(2,1)S(1)}, u32[]{:S(2)}, u32[]{:S(2)}) collective-permute-start(bf16[32,256]{1,0:T(8,128)(2,1)S(1)} %get-tuple-element.87), channel_id=1, source_target_pairs={{16,0},{32,16},{48,32},{64,48},{80,64},{96,80},{112,96},{0,112},{1... | collective-permute-start | bytes 49160 | tf_op jit(solution)/shard_map/ppermute | solution.py:441
  54.5 18.1 %collective-permute-start.12 = (bf16[640,512]{1,0:T(8,128)(2,1)S(1)}, bf16[640,512]{1,0:T(8,128)(2,1)S(1)}, u32[]{:S(2)}, u32[]{:S(2)}) collective-permute-start(bf16[640,512]{1,0:T(8,128)(2,1)S(1)} %get-tuple-element.106), channel_id=1, source_target_pairs={{0,16},{16,0},{1,17},{17,1},{2,18},{18,2},{3,19},{19,3},{4,20},{20... | collective-permute-start | bytes 1966088 | tf_op jit(solution)/shard_map/ppermute | solution.py:448
  72.0 3.0 %copy-start.20 = (bf16[227,2048]{1,0:T(8,128)(2,1)}, bf16[227,2048]{1,0:T(8,128)(2,1)S(1)}, u32[]{:S(2)}) copy-start(bf16[227,2048]{1,0:T(8,128)(2,1)S(1)} %get-tuple-element.104.refs_2_) | copy-start | bytes 2789380
  72.0 2.7 %collective-permute-start.13 = (bf16[896,512]{1,0:T(8,128)(2,1)S(1)}, bf16[896,512]{1,0:T(8,128)(2,1)S(1)}, u32[]{:S(2)}, u32[]{:S(2)}) collective-permute-start(bf16[896,512]{1,0:T(8,128)(2,1)S(1)} %get-tuple-element.108), channel_id=1, source_target_pairs={{0,16},{16,0},{1,17},{17,1},{2,18},{18,2},{3,19},{19,3},{4,20},{20... | collective-permute-start | bytes 2752520 | tf_op jit(solution)/shard_map/ppermute | solution.py:448
  100.8 5.1 %collective-permute-start.14 = (bf16[96,512]{1,0:T(8,128)(2,1)S(1)}, bf16[96,512]{1,0:T(8,128)(2,1)S(1)}, u32[]{:S(2)}, u32[]{:S(2)}) collective-permute-start(bf16[96,512]{1,0:T(8,128)(2,1)S(1)} %reduce_sum.12), channel_id=1, source_target_pairs={{0,64},{32,96},{64,0},{96,32},{1,65},{33,97},{65,1},{97,33},{2,66}... | collective-permute-start | bytes 294920 | tf_op jit(solution)/shard_map/ppermute | solution.py:535
  101.5 5.4 %collective-permute-start.15 = (bf16[96,512]{1,0:T(8,128)(2,1)S(1)}, bf16[96,512]{1,0:T(8,128)(2,1)S(1)}, u32[]{:S(2)}, u32[]{:S(2)}) collective-permute-start(bf16[96,512]{1,0:T(8,128)(2,1)S(1)} %reduce_sum.12), channel_id=1, source_target_pairs={{0,32},{32,64},{64,96},{96,0},{1,33},{33,65},{65,97},{97,1},{2,34}... | collective-permute-start | bytes 294920 | tf_op jit(solution)/shard_map/ppermute | solution.py:535
  103.9 4.3 %collective-permute-start.16 = (bf16[96,512]{1,0:T(8,128)(2,1)S(1)}, bf16[96,512]{1,0:T(8,128)(2,1)S(1)}, u32[]{:S(2)}, u32[]{:S(2)}) collective-permute-start(bf16[96,512]{1,0:T(8,128)(2,1)S(1)} %reduce_sum.12), channel_id=1, source_target_pairs={{0,96},{32,0},{64,32},{96,64},{1,97},{33,1},{65,33},{97,65},{2,98}... | collective-permute-start | bytes 294920 | tf_op jit(solution)/shard_map/ppermute | solution.py:535
  109.7 26.5 %all-to-all-start.1 = ((bf16[16,96,512]{2,1,0:T(8,128)(2,1)}), bf16[16,96,512]{2,1,0:T(8,128)(2,1)S(1)}, u32[]{:S(2)}, u32[]{:S(2)}) async-start(bf16[16,96,512]{2,1,0:T(8,128)(2,1)} %broadcast_in_dim.2), calls=%async_computation.1 | async-start | bytes 3145728 | tf_op jit(solution)/shard_map/all_to_all | solution.py:540
  113.4 7.4 %collective-permute-start.17 = (bf16[227,128]{1,0:T(8,128)(2,1)S(1)}, bf16[227,128]{1,0:T(8,128)(2,1)S(1)}, u32[]{:S(2)}, u32[]{:S(2)}) collective-permute-start(bf16[227,128]{1,0:T(8,128)(2,1)S(1)} %get-tuple-element.114.refs_8_), channel_id=1, source_target_pairs={{0,16},{16,32},{32,48},{48,64},{64,80},{80,96},{96,112},{112,0},{1... | collective-permute-start | bytes 174344 | tf_op jit(solution)/shard_map/ppermute | solution.py:440
  115.5 5.3 %collective-permute-start.18 = (bf16[227,128]{1,0:T(8,128)(2,1)S(1)}, bf16[227,128]{1,0:T(8,128)(2,1)S(1)}, u32[]{:S(2)}, u32[]{:S(2)}) collective-permute-start(bf16[227,128]{1,0:T(8,128)(2,1)S(1)} %get-tuple-element.115.refs_7_), channel_id=1, source_target_pairs={{16,0},{32,16},{48,32},{64,48},{80,64},{96,80},{112,96},{0,112},{1... | collective-permute-start | bytes 174344 | tf_op jit(solution)/shard_map/ppermute | solution.py:441
  115.8 20.3 %collective-permute-start.19 = (bf16[227,128]{1,0:T(8,128)(2,1)S(1)}, bf16[227,128]{1,0:T(8,128)(2,1)S(1)}, u32[]{:S(2)}, u32[]{:S(2)}) collective-permute-start(bf16[227,128]{1,0:T(8,128)(2,1)S(1)} %get-tuple-element.116), channel_id=1, source_target_pairs={{0,1},{1,2},{2,3},{3,4},{4,5},{5,6},{6,7},{7,8},{8,9},{9,10},{10,1... | collective-permute-start | bytes 174344 | tf_op jit(solution)/shard_map/ppermute | solution.py:442
  117.3 18.8 %collective-permute-start.20 = (bf16[227,128]{1,0:T(8,128)(2,1)S(1)}, bf16[227,128]{1,0:T(8,128)(2,1)S(1)}, u32[]{:S(2)}, u32[]{:S(2)}) collective-permute-start(bf16[227,128]{1,0:T(8,128)(2,1)S(1)} %get-tuple-element.117), channel_id=1, source_target_pairs={{1,0},{2,1},{3,2},{4,3},{5,4},{6,5},{7,6},{8,7},{9,8},{10,9},{11,1... | collective-permute-start | bytes 174344 | tf_op jit(solution)/shard_map/ppermute | solution.py:443
  136.1 8.0 %collective-permute-start.21 = (bf16[1536,512]{1,0:T(8,128)(2,1)S(1)}, bf16[1536,512]{1,0:T(8,128)(2,1)S(1)}, u32[]{:S(2)}, u32[]{:S(2)}) collective-permute-start(bf16[1536,512]{1,0:T(8,128)(2,1)S(1)} %bitcast.7), channel_id=1, source_target_pairs={{0,16},{16,0},{1,17},{17,1},{2,18},{18,2},{3,19},{19,3},{4,20},{20... | collective-permute-start | bytes 4718600 | tf_op jit(solution)/shard_map/ppermute | solution.py:448
  138.4 1.2 copy-start.21
